TPU v7x, 32 devices: a whole 2x2x4 slice. The times are simulated.
32 devices in a mesh: grp: 4 (over z), pb: 8 (over y, x, core).
Axes of the slice: x: 2, y: 2, z: 4, core: 2. Of those that a mesh axis runs over, the one named last changes fastest.
Arguments:
- queries: bfloat16 [2048, 4096], P('grp', 'pb'), may hold values from -12 to 12
- outputs: bfloat16 [2048, 4096], P('grp', 'pb'), may hold values from -3 to 3
- readout_grad: bfloat16 [2048, 8192], P('grp', 'pb'), may hold values from -24 to 24
- readout_weight: bfloat16 [4096, 8192], P('pb'), may hold values from -0.09375 to 0.09375
- log_norm: float32 [2048, 32], P('grp', 'pb'), may hold values from 9 to 11
- probes: int32 [32, 2048, 4], P('pb', 'grp'), may hold values from 0 to 31, all different within a row; in each aligned block of 512 rows (0 to 511, 512 to 1023, ..., all dimensions but the last counted through in order) at most 128 rows name the same one
- owner_slots: int32 [32, 32], P('pb'), may hold values from 0 to 31, each once within a row
- counts: int32 [32, 32], P('pb', 'grp'), may hold values from 1 to 512
- cluster_keys: bfloat16 [32, 32, 512, 128], P('pb', 'grp'), may hold values from -6 to 6
- values: bfloat16 [32, 32, 512, 128], P('pb', 'grp'), may hold values from -6 to 6
Outputs:
- query_grad: bfloat16 [2048, 4096], P('grp', 'pb')
Inputs may be any that keep to these rules, and one draw needn't show every extreme that they name: `probes`: each token names 4 different clusters for each head. Within the 512 tokens of one index of grp and one head, no cluster is named by more than 128 tokens, a bound that some block reaches. `owner_slots`: for each head a permutation of the 32 clusters; slot s is stored on index s // 8 of grp.
All inputs are finite; a program needn't handle non-finite values.
Results may differ from a plain program's by a relative error of at most 0.029.
Values may be sent and summed in bfloat16 or wider, within the bound.
A program may use at most 128 MiB of HBM per device.

v0:
```python
import jax
import jax.numpy as jnp
from jax import lax
from jax.sharding import PartitionSpec as P


def slot_places(probe_ids, slot_table, capacity):
    cluster_ids = jnp.arange(slot_table.shape[1], dtype=jnp.int32)
    matches = probe_ids[..., None] == cluster_ids
    slot_ids = jnp.sum(jnp.where(matches, slot_table[:, None, None, :], 0), axis=3, dtype=jnp.int32)
    same_slot = slot_ids[..., None] == cluster_ids
    marked = jnp.sum(same_slot.astype(jnp.int32), axis=2, dtype=jnp.int32)
    before = jnp.cumsum(marked, axis=1, dtype=jnp.int32) - marked
    ranking = jnp.sum(jnp.where(same_slot, before[:, :, None, :], 0), axis=3, dtype=jnp.int32)
    return slot_ids * capacity + ranking


def to_slots(rows, places, slot_total):
    head_count, token_count, probe_count = places.shape
    repeated = jnp.repeat(rows, probe_count, axis=1)
    flat_places = places.reshape(head_count, token_count * probe_count)
    blank_rows = jnp.zeros((head_count, slot_total) + rows.shape[2:], rows.dtype)

    def place_head(blank_head, place_head_ids, rows_head):
        return blank_head.at[place_head_ids].set(rows_head)

    return jax.vmap(place_head)(blank_rows, flat_places, repeated)


def shards(
    queries,
    outputs,
    readout_grad,
    readout_weight,
    log_norm,
    probes,
    owner_slots,
    counts,
    cluster_keys,
    values,
):
    token_count = queries.shape[0]
    head_count = probes.shape[0]
    probe_count = probes.shape[2]
    local_clusters = cluster_keys.shape[1]
    cluster_span = cluster_keys.shape[2]
    head_width = cluster_keys.shape[3]
    clusters = owner_slots.shape[1]
    groups = lax.axis_size("grp")
    capacity = 2 * token_count * probe_count // clusters
    slot_total = clusters * capacity
    score_scale = head_width ** (-0.5)
    places = slot_places(probes, owner_slots, capacity)

    def shaped(rows):
        return to_slots(rows, places, slot_total).reshape(
            (head_count, clusters, capacity) + rows.shape[2:]
        )

    query_slots = shaped(queries.reshape(token_count, head_count, head_width).transpose(1, 0, 2))
    norm_slots = shaped(log_norm.T[:, :, None])[..., 0]
    grad_out = lax.dot_general(
        lax.all_gather(readout_grad, "pb", axis=1, tiled=True),
        readout_weight,
        (((1,), (1,)), ((), ())),
        preferred_element_type=jnp.float32,
    ).astype(jnp.bfloat16)
    row_delta = jnp.sum(
        (grad_out.astype(jnp.float32) * outputs.astype(jnp.float32)).reshape(
            token_count, head_count, head_width
        ),
        axis=2,
    )
    grad_slots = shaped(grad_out.reshape(token_count, head_count, head_width).transpose(1, 0, 2))
    delta_slots = shaped(row_delta.T[:, :, None])[..., 0]
    grad_slots, delta_slots = (grad_slots, delta_slots)
    query_recv, grad_recv = (
        lax.all_to_all(query_slots, "grp", split_axis=1, concat_axis=2, tiled=True),
        lax.all_to_all(grad_slots, "grp", split_axis=1, concat_axis=2, tiled=True),
    )
    norm_recv, delta_recv = (
        lax.all_to_all(norm_slots, "grp", split_axis=1, concat_axis=2, tiled=True),
        lax.all_to_all(delta_slots, "grp", split_axis=1, concat_axis=2, tiled=True),
    )
    arrivals = groups * capacity
    key_index = jnp.arange(cluster_span, dtype=jnp.int32)
    contract_last = (((1,), (1,)), ((), ()))

    def block_grad(pieces):
        query_block, grad_block, norm_block, delta_block, key_block, value_block, valid = pieces
        scores = (
            lax.dot_general(
                query_block, key_block, contract_last, preferred_element_type=jnp.float32
            )
            * score_scale
        )
        weights = jnp.where(
            key_index[None, :] < valid,
            jnp.exp(scores - norm_block[:, None]),
            jnp.zeros_like(scores),
        )
        grad_prob = lax.dot_general(
            grad_block, value_block, contract_last, preferred_element_type=jnp.float32
        )
        grad_score = (weights * (grad_prob - delta_block[:, None])).astype(jnp.bfloat16)
        return (
            jnp.dot(grad_score, key_block, preferred_element_type=jnp.float32) * score_scale
        ).astype(jnp.bfloat16)

    block_count = head_count * local_clusters
    partials = lax.map(
        block_grad,
        (
            query_recv.reshape(block_count, arrivals, head_width),
            grad_recv.reshape(block_count, arrivals, head_width),
            norm_recv.reshape(block_count, arrivals),
            delta_recv.reshape(block_count, arrivals),
            cluster_keys.reshape(block_count, cluster_span, head_width),
            values.reshape(block_count, cluster_span, head_width),
            counts.reshape(block_count),
        ),
    )
    returned = lax.all_to_all(
        partials.reshape(head_count, local_clusters, arrivals, head_width),
        "grp",
        split_axis=2,
        concat_axis=1,
        tiled=True,
    )
    returned = returned.reshape(head_count, slot_total, head_width)

    def pick_head(returned_head, place_head_ids):
        return returned_head[place_head_ids]

    picked = jax.vmap(pick_head)(returned, places.reshape(head_count, token_count * probe_count))
    summed = jnp.sum(
        picked.reshape(head_count, token_count, probe_count, head_width).astype(jnp.float32), axis=2
    )
    return (
        summed.astype(jnp.bfloat16).transpose(1, 0, 2).reshape(token_count, head_count * head_width)
    )


def solution(mesh):
    placed = (
        P("grp", "pb"),
        P("grp", "pb"),
        P("grp", "pb"),
        P("pb", None),
        P("grp", "pb"),
        P("pb", "grp", None),
        P("pb", None),
        P("pb", "grp"),
        P("pb", "grp", None, None),
        P("pb", "grp", None, None),
    )
    return jax.shard_map(
        shards, mesh=mesh, in_specs=placed, out_specs=P("grp", "pb"), check_vma=False
    )
```

profile of v0, /device:TPU:0, one launch (start us, length us, event | category | flops | bytes accessed | tf_op | source)
XLA Modules:
  0.0 686.9 jit_solution(1616857188020381947)
XLA Ops:
  8.5 4.6 reduce-window.6
  16.4 30.5 %scatter_custom_fusion.1 = f32[16384]{0:T(1024)S(1)} fusion(s32[8192]{0:T(1024)S(1)} %bitcast.134, f32[8192]{0:T(1024)S(1)} %reshape.194, f32[]{:T(128)} %constant.36.clone.1), kind=kCustom, calls=%fused_computation.63 | custom fusion | bytes 65540
  47.6 6.3 all-to-all-start.1
  54.6 23.7 %scatter_custom_fusion = bf16[16384,128]{1,0:T(8,128)(2,1)} fusion(s32[8192]{0:T(1024)S(1)} %bitcast.135, bf16[8192,128]{1,0:T(8,128)(2,1)S(1)} %bitcast.120, bf16[]{:T(256)} %constant.24.clone.1), kind=kCustom, calls=%fused_computation.40 | custom fusion | bytes 4194306
  78.3 4.7 copy.76
  83.1 5.2 all-to-all-start
  88.6 10.3 %bitcast_reduce_fusion = (f32[512,4]{0,1:T(4,128)S(1)}, bf16[512,512]{0,1:T(8,128)(2,1)S(1)}) fusion(bf16[512,512]{0,1:T(8,128)(2,1)S(1)} %copy.85, bf16[512,8192]{1,0:T(8,128)(2,1)} %all-gather.2.cloned.1.call-done, bf16[512,8192]{1,0:T(8,128)(2,1)} %param.15), kind=kOutput, calls=%fused_computation.43 | convolution fusion | flops 4296275968 | bytes 17833984 | tf_op jit(solution)/shard_map/dot_general | solution.py:62
  99.9 30.5 %scatter_custom_fusion.3 = f32[16384]{0:T(1024)S(1)} fusion(s32[8192]{0:T(1024)S(1)} %bitcast.136, f32[8192]{0:T(1024)S(1)} %reshape.210, f32[]{:T(128)} %constant.36.clone.1), kind=kCustom, calls=%fused_computation.61 | custom fusion | bytes 65540
  131.0 50.4 %all-to-all-done = bf16[4,32,128,128]{3,2,0,1:T(8,128)(2,1)} async-done(((bf16[4,32,128,128]{3,2,0,1:T(8,128)(2,1)}), bf16[4,32,128,128]{3,2,0,1:T(8,128)(2,1)}, u32[]{:S(2)}, u32[]{:S(2)}) %all-to-all-start) | async-done | bytes 4194336 | tf_op jit(solution)/shard_map/all_to_all | solution.py:78
  181.4 3.3 all-to-all-start.3
  185.6 23.6 %scatter_custom_fusion.2 = bf16[16384,128]{1,0:T(8,128)(2,1)} fusion(s32[8192]{0:T(1024)S(1)} %bitcast.137, bf16[8192,128]{1,0:T(8,128)(2,1)S(1)} %bitcast.119, bf16[]{:T(256)} %constant.24.clone.1), kind=kCustom, calls=%fused_computation.38 | custom fusion | bytes 4194306
  209.2 4.7 copy.82
  214.0 5.2 all-to-all-start.2
  219.3 4.7 copy.78
  224.0 87.9 %all-to-all-done.2 = bf16[4,32,128,128]{3,2,0,1:T(8,128)(2,1)} async-done(((bf16[4,32,128,128]{3,2,0,1:T(8,128)(2,1)}), bf16[4,32,128,128]{3,2,0,1:T(8,128)(2,1)}, u32[]{:S(2)}, u32[]{:S(2)}) %all-to-all-start.2) | async-done | bytes 4194336 | tf_op jit(solution)/shard_map/all_to_all | solution.py:79
  311.9 4.7 copy.84
  316.6 152.8 %while.11 = (s32[]{:T(128)}, bf16[32,512,128]{2,1,0:T(8,128)(2,1)}, s32[32]{0:T(128)S(1)}, bf16[32,512,128]{2,1,0:T(8,128)(2,1)}, bf16[32,512,128]{2,1,0:T(8,128...) while((s32[]{:T(128)}, bf16[32,512,128]{2,1,0:T(8,128)(2,1)}, ...), condition=%wide.region_11.12_spmd.clone, body=%wide.region_10.11_spmd.clone.sunk | while | flops 203031040 | bytes 2900089 | solution.py:111
  319.2 2.2 fusion.56
  338.2 2.2 fusion.56
  343.0 2.2 fusion.56
  357.4 2.2 fusion.56
  362.1 2.2 fusion.56
  390.8 2.2 fusion.56
  409.9 2.2 fusion.56
  443.3 2.2 fusion.56
  467.2 2.2 fusion.56
  469.4 6.9 copy.105
  476.3 4.9 all-to-all-start.4
  481.2 92.7 %all-to-all-done.4 = bf16[4,8,512,128]{3,1,0,2:T(8,128)(2,1)} async-done(((bf16[4,8,512,128]{3,1,0,2:T(8,128)(2,1)}), bf16[4,8,512,128]{3,1,0,2:T(8,128)(2,1)}, u32[]{:S(2)}, u32[]{:S(2)}) %all-to-all-start.4) | async-done | bytes 4194336 | tf_op jit(solution)/shard_map/all_to_all | solution.py:123
  573.9 5.8 copy.90
  579.7 96.3 %gather_fusion = bf16[8192,128]{1,0:T(8,128)(2,1)S(1)} fusion(bf16[4,4096,128]{2,1,0:T(8,128)(2,1)} %bitcast.112, s32[8192]{0:T(1024)S(1)} %bitcast.111), kind=kCustom, calls=%fused_computation | custom fusion | bytes 4259840 | tf_op jit(solution)/shard_map/vmap()/gather | solution.py:133
  676.0 2.8 reduce_sum.52
  (204 shorter events, 142.6 us)
Async XLA Ops:
  6.5 8.6 %copy-start.5 = (s32[2]{0:T(128)S(1)}, s32[2]{0:T(128)}, u32[]{:S(2)}) copy-start(s32[2]{0:T(128)} %constant.43) | copy-start | bytes 28
  6.5 8.7 %copy-start.4 = (s32[2]{0:T(128)S(1)}, s32[2]{0:T(128)}, u32[]{:S(2)}) copy-start(s32[2]{0:T(128)} %constant.46) | copy-start | bytes 28
  6.5 8.9 %copy-start.2 = (f32[512,4]{0,1:T(4,128)S(1)}, f32[512,4]{0,1:T(4,128)}, u32[]{:S(2)}) copy-start(f32[512,4]{0,1:T(4,128)} %param.16) | copy-start | bytes 24580
  6.5 82.0 %all-gather.2.cloned.1.call-start = ((), (), s32[]{:S(2)}) async-start(), calls=%async_computation.5 | async-start | bytes 9437184 | tf_op jit(solution)/shard_map/all_gather | solution.py:63
  7.3 46.6 %copy-start = (bf16[512,512]{1,0:T(8,128)(2,1)S(1)}, bf16[512,512]{1,0:T(8,128)(2,1)}, u32[]{:S(2)}) copy-start(bf16[512,512]{1,0:T(8,128)(2,1)} %param.12) | copy-start | bytes 1572868
  47.6 35.5 %all-to-all-start.1 = ((f32[4,32,128]{2,0,1:T(4,128)}), f32[4,32,128]{2,0,1:T(4,128)S(1)}, u32[]{:S(2)}, u32[]{:S(2)}) async-start(f32[4,32,128]{2,0,1:T(4,128)} %copy.79), calls=%async_computation.1 | async-start | bytes 131072 | tf_op jit(solution)/shard_map/all_to_all | solution.py:82
  83.1 5.3 copy-start.1
  83.1 98.4 %all-to-all-start = ((bf16[4,32,128,128]{3,2,0,1:T(8,128)(2,1)}), bf16[4,32,128,128]{3,2,0,1:T(8,128)(2,1)}, u32[]{:S(2)}, u32[]{:S(2)}) async-start(bf16[4,32,128,128]{3,2,0,1:T(8,128)(2,1)} %copy.76), calls=%async_computation | async-start | bytes 8388608 | tf_op jit(solution)/shard_map/all_to_all | solution.py:78
  181.4 32.5 %all-to-all-start.3 = ((f32[4,32,128]{2,0,1:T(4,128)}), f32[4,32,128]{2,0,1:T(4,128)S(1)}, u32[]{:S(2)}, u32[]{:S(2)}) async-start(f32[4,32,128]{2,0,1:T(4,128)} %copy.86), calls=%async_computation.3 | async-start | bytes 131072 | tf_op jit(solution)/shard_map/all_to_all | solution.py:83
  214.0 5.2 copy-start.3
  214.0 97.9 %all-to-all-start.2 = ((bf16[4,32,128,128]{3,2,0,1:T(8,128)(2,1)}), bf16[4,32,128,128]{3,2,0,1:T(8,128)(2,1)}, u32[]{:S(2)}, u32[]{:S(2)}) async-start(bf16[4,32,128,128]{3,2,0,1:T(8,128)(2,1)} %copy.82), calls=%async_computation.2 | async-start | bytes 8388608 | tf_op jit(solution)/shard_map/all_to_all | solution.py:79
  476.3 97.6 %all-to-all-start.4 = ((bf16[4,8,512,128]{3,1,0,2:T(8,128)(2,1)}), bf16[4,8,512,128]{3,1,0,2:T(8,128)(2,1)}, u32[]{:S(2)}, u32[]{:S(2)}) async-start(bf16[4,8,512,128]{3,1,0,2:T(8,128)(2,1)} %bitcast.113), calls=%async_computation.4 | async-start | bytes 8388608 | tf_op jit(solution)/shard_map/all_to_all | solution.py:123
Sparse Core Ops, SparseCore 0:
  9.3 57.0 all-gather.1
where the time goes:
time: 690 us; the launch traced here: 687 us
  local copies, waits for them, and re-layouts  263 us (38%)
  waiting for transfers between devices  232 us (34%)
  matrix products  123 us (18%)
  other arithmetic  30.1 us (4%)
  starting transfers between devices  24.9 us (4%)
  between operations  13.7 us (2%)
    unnamed x19, local copies, waits for them, and re-layouts  109 us
    gather x1, local copies, waits for them, and re-layouts, pick_head(): return returned_head[place_head_ids]  96.3 us
    all_to_all x1, waiting for transfers between devices, shards(): lax.all_to_all(partials.reshape(head_count, local_clusters, arrivals, hea...  92.7 us
    all_to_all x1, waiting for transfers between devices, shards(): lax.all_to_all(grad_slots, 'grp', split_axis=1, concat_axis=2, tiled=True)  87.9 us
    dot_general x32, matrix products, block_grad(): jnp.dot(grad_score, key_block, preferred_element_type=jnp.float32)  71.6 us
    all_to_all x1, waiting for transfers between devices, shards(): lax.all_to_all(query_slots, 'grp', split_axis=1, concat_axis=2, tiled=True)  50.4 us
    dot_general x32, matrix products, block_grad(): lax.dot_general(grad_block, value_block, contract_last, preferred_element...  40.7 us
    lt x32, other arithmetic, block_grad(): key_index[None, :] < valid  20.8 us
  transfers between devices with their start and end apart: 6, of which 3 were waited for; matrix products, arithmetic and copies ran while one was open for 21% of the time, Pallas kernels for 0%

commit v1 on v0

v1 whole, which is shorter than its diff:
```python
import functools

import jax
import jax.numpy as jnp
from jax import lax
from jax.experimental import pallas as pl
from jax.experimental.pallas import tpu as pltpu
from jax.sharding import PartitionSpec as P

LANES = 128
AUX = 8
PAIR = 2


def three_parts(x):
    high = lax.reduce_precision(x, 8, 7)
    rest = x - high
    middle = lax.reduce_precision(rest, 8, 7)
    return jnp.stack([high, middle, rest - middle], axis=-1)


def probe_ranks(probes, owner_slots, local_clusters, token_count, groups):
    me = lax.axis_index("grp")
    clusters = owner_slots.shape[1]
    cluster_ids = jnp.arange(clusters, dtype=jnp.int32)
    slots = me * local_clusters + jnp.arange(local_clusters, dtype=jnp.int32)
    named = jnp.sum(
        jnp.where(owner_slots[:, None, :] == slots[None, :, None], cluster_ids, 0), axis=2, dtype=jnp.int32
    )
    marked = jnp.any(probes[:, None, :, :] == named[:, :, None, None], axis=3)
    marked = marked.reshape(probes.shape[0], local_clusters, groups, token_count)
    earlier = jnp.arange(token_count)[:, None] < jnp.arange(token_count)[None, :]
    before = lax.dot_general(
        marked.astype(jnp.bfloat16),
        earlier.astype(jnp.bfloat16),
        (((3,), (0,)), ((), ())),
        preferred_element_type=jnp.float32,
    )
    return jnp.where(marked, before.astype(jnp.int32), -1)


def grad_kernel(groups, capacity, scale, counts, q, g, aux, rows, cols, keys, values, out, total):
    head, step = pl.program_id(0), pl.program_id(1)
    token_count = q.shape[0] // groups
    span = keys.shape[2]
    lane = lax.broadcasted_iota(jnp.int32, (span, LANES), 1)
    key_id = lax.broadcasted_iota(jnp.int32, (span, LANES), 0)
    own = lane - head * AUX
    ones = jnp.where((own >= 0) & (own < 3), 1.0, 0.0)
    value_side = jnp.where((own >= 3) & (own < 6), 1.0, 0.0).astype(jnp.bfloat16)
    place = lax.broadcasted_iota(jnp.int32, (capacity, token_count), 0)
    contract_last = (((1,), (1,)), ((), ()))
    partials = []
    for i in range(PAIR):
        valid = counts[head, step * PAIR + i]
        key_side = jnp.where((lane == LANES - 1) & (key_id >= valid), -1e30, ones).astype(jnp.bfloat16)
        key_block, value_block = keys[0, i], values[0, i]
        picked = []
        for group in range(groups):
            span_of = pl.ds(group * token_count, token_count)
            chosen = (rows[0, i, :, span_of] == place).astype(jnp.bfloat16)
            rhs = jnp.concatenate([q[span_of, :], aux[span_of, :], g[span_of, :]], axis=1)
            picked.append(jnp.dot(chosen, rhs, preferred_element_type=jnp.float32).astype(jnp.bfloat16))
        picked = jnp.concatenate(picked, axis=0)
        scores = lax.dot_general(
            picked[:, : 2 * LANES],
            jnp.concatenate([key_block, key_side], axis=1),
            contract_last,
            preferred_element_type=jnp.float32,
        )
        grad_prob = lax.dot_general(
            picked[:, LANES:],
            jnp.concatenate([value_side, value_block], axis=1),
            contract_last,
            preferred_element_type=jnp.float32,
        )
        grad_score = (jnp.exp(scores * scale) * grad_prob).astype(jnp.bfloat16)
        partials.append(jnp.dot(grad_score, key_block, preferred_element_type=jnp.float32).astype(jnp.bfloat16))
    spot = lax.broadcasted_iota(jnp.int32, (token_count, capacity), 1)
    for group in range(groups):
        span_of = pl.ds(group * token_count, token_count)
        chosen = jnp.concatenate(
            [(cols[0, 0, span_of, i : i + 1] == spot).astype(jnp.bfloat16) for i in range(PAIR)], axis=1
        )
        part = jnp.concatenate([p[group * capacity : (group + 1) * capacity] for p in partials], axis=0)
        add = jnp.dot(chosen, part, preferred_element_type=jnp.float32)

        @pl.when(step == 0)
        def _():
            total[span_of, :] = add

        @pl.when(step > 0)
        def _():
            total[span_of, :] += add

    @pl.when(step == pl.num_programs(1) - 1)
    def _():
        out[...] = (total[...] * scale).astype(out.dtype)


def shards(
    queries, outputs, readout_grad, readout_weight, log_norm, probes, owner_slots, counts, cluster_keys, values
):
    token_count = queries.shape[0]
    heads, local_clusters, span, width = cluster_keys.shape
    clusters = owner_slots.shape[1]
    groups = lax.axis_size("grp")
    capacity = 2 * token_count * probes.shape[2] // clusters
    scale = width ** (-0.5)
    every = groups * token_count

    all_probes = lax.all_gather(probes, "grp", axis=1, tiled=True)
    all_queries = lax.all_gather(queries, "grp", axis=0, tiled=True)
    ranks = probe_ranks(all_probes, owner_slots, local_clusters, token_count, groups)
    ranks = ranks.reshape(heads, local_clusters, 1, every)
    steps = local_clusters // PAIR
    rank_cols = ranks.reshape(heads, steps, PAIR, every).transpose(0, 1, 3, 2)

    grad_out = lax.dot_general(
        lax.all_gather(readout_grad, "pb", axis=1, tiled=True),
        readout_weight,
        (((1,), (1,)), ((), ())),
        preferred_element_type=jnp.float32,
    ).astype(jnp.bfloat16)
    row_delta = jnp.sum(
        (grad_out.astype(jnp.float32) * outputs.astype(jnp.float32)).reshape(token_count, heads, width), axis=2
    )
    aux = jnp.concatenate(
        [three_parts(log_norm * (-1.0 / scale)), three_parts(-row_delta), jnp.zeros((token_count, heads, 2))], axis=2
    ).reshape(token_count, heads * AUX)
    aux = jnp.concatenate(
        [aux, jnp.zeros((token_count, LANES - 1 - heads * AUX)), jnp.ones((token_count, 1))], axis=1
    ).astype(jnp.bfloat16)
    all_grads = lax.all_gather(jnp.concatenate([grad_out, aux], axis=1), "grp", axis=0, tiled=True)

    partial = pl.pallas_call(
        functools.partial(grad_kernel, groups, capacity, scale),
        grid=(heads, steps),
        in_specs=[
            pl.BlockSpec(memory_space=pltpu.SMEM),
            pl.BlockSpec((every, width), lambda h, c: (0, h)),
            pl.BlockSpec((every, width), lambda h, c: (0, h)),
            pl.BlockSpec((every, LANES), lambda h, c: (0, heads)),
            pl.BlockSpec((1, PAIR, 1, every), lambda h, c: (h, c, 0, 0)),
            pl.BlockSpec((1, 1, every, PAIR), lambda h, c: (h, c, 0, 0)),
            pl.BlockSpec((1, PAIR, span, width), lambda h, c: (h, c, 0, 0)),
            pl.BlockSpec((1, PAIR, span, width), lambda h, c: (h, c, 0, 0)),
        ],
        out_specs=pl.BlockSpec((every, width), lambda h, c: (0, h)),
        out_shape=jax.ShapeDtypeStruct((every, heads * width), jnp.bfloat16),
        scratch_shapes=[pltpu.VMEM((every, width), jnp.float32)],
        compiler_params=pltpu.CompilerParams(vmem_limit_bytes=50 * 2**20),
    )(counts, all_queries, all_grads, all_grads, ranks, rank_cols, cluster_keys, values)
    returned = lax.all_to_all(
        partial.reshape(groups, token_count, heads * width), "grp", split_axis=0, concat_axis=0, tiled=True
    )
    return jnp.sum(returned.astype(jnp.float32), axis=0).astype(jnp.bfloat16)


def solution(mesh):
    placed = (
        P("grp", "pb"),
        P("grp", "pb"),
        P("grp", "pb"),
        P("pb", None),
        P("grp", "pb"),
        P("pb", "grp", None),
        P("pb", None),
        P("pb", "grp"),
        P("pb", "grp", None, None),
        P("pb", "grp", None, None),
    )
    return jax.shard_map(shards, mesh=mesh, in_specs=placed, out_specs=P("grp", "pb"), check_vma=False)
```

time: 690 us -> 284 us (0.41)
  local copies, waits for them, and re-layouts: 263 us -> 10.3 us
  matrix products: 123 us -> 10.6 us
  waiting for transfers between devices: 232 us -> 126 us
  blocking collectives: 0 us -> 65.2 us
  Pallas kernels: 0 us -> 54.2 us
  other arithmetic: 30.1 us -> 4.04 us
  starting transfers between devices: 24.9 us -> 0.08 us
    all_to_all x5 -> x0, waiting for transfers between devices: 231 us -> none  [the longest x1 92.7 us: shards(): lax.all_to_all(partials.reshape(head_count, local_clusters, arrivals, hea...]
    dot_general x64 -> x1, matrix products: 112 us -> 0.25 us  [probe_ranks(): lax.dot_general(marked.astype(jnp.bfloat16), earlier.astype(jnp.bfloat16)...]
    unnamed x19 -> x7, local copies, waits for them, and re-layouts: 109 us -> 0.13 us
    gather x1 -> x0, local copies, waits for them, and re-layouts: 96.3 us -> none  [pick_head(): return returned_head[place_head_ids]]
    all_gather x0 -> x2, waiting for transfers between devices: none -> 67.5 us  [the longest x1 55.2 us: shards(): lax.all_gather(jnp.concatenate([grad_out, aux], axis=1), 'grp', axis=0, t...]
    all_gather x1, waiting for transfers between devices: 0.02 us -> 57.4 us  [shards(): lax.all_gather(readout_grad, 'pb', axis=1, tiled=True)]
    pallas_call x0 -> x1, Pallas kernels: none -> 54.2 us  [shards(): pl.pallas_call(functools.partial(grad_kernel, groups, capacity, scale), g...]
    all_to_all x0 -> x1, blocking collectives: none -> 50.9 us  [shards(): lax.all_to_all(partial.reshape(groups, token_count, heads * width), 'grp'...]
  transfers between devices with their start and end apart: 6 -> 3, of which waited for: 3 -> 3; matrix products, arithmetic and copies ran while one was open for 21% -> 8% of each run, Pallas kernels for 0% -> 0%
where the time goes in v1:
time: 284 us
  waiting for transfers between devices  126 us (44%)
  blocking collectives  65.2 us (23%)
  Pallas kernels  54.2 us (19%)
  between operations  13.3 us (5%)
  matrix products  10.6 us (4%)
  local copies, waits for them, and re-layouts  10.3 us (4%)
  other arithmetic  4.04 us (1%)
    all_gather x1, waiting for transfers between devices, shards(): lax.all_gather(readout_grad, 'pb', axis=1, tiled=True)  57.4 us
    all_gather x1, waiting for transfers between devices, shards(): lax.all_gather(jnp.concatenate([grad_out, aux], axis=1), 'grp', axis=0, t...  55.2 us
    pallas_call x1, Pallas kernels, shards(): pl.pallas_call(functools.partial(grad_kernel, groups, capacity, scale), g...  54.2 us
    all_to_all x1, blocking collectives, shards(): lax.all_to_all(partial.reshape(groups, token_count, heads * width), 'grp'...  50.9 us
    all_gather x1, blocking collectives, shards(): all_probes = lax.all_gather(probes, 'grp', axis=1, tiled=True)  14.3 us
    all_gather x1, waiting for transfers between devices, shards(): all_queries = lax.all_gather(queries, 'grp', axis=0, tiled=True)  12.3 us
    dot_general x1, matrix products, shards(): lax.dot_general(lax.all_gather(readout_grad, 'pb', axis=1, tiled=True), r...  10.3 us
    another operation x2, local copies, waits for them, and re-layouts, shards(): rank_cols = ranks.reshape(heads, steps, PAIR, every).transpose(0, 1, 3, 2)  8.86 us
  transfers between devices with their start and end apart: 3, of which 3 were waited for; matrix products, arithmetic and copies ran while one was open for 8% of the time, Pallas kernels for 0%

profile of v1, /device:TPU:0, one launch (start us, length us, event | category | flops | bytes accessed | tf_op | source)
XLA Modules:
  0.0 284.0 jit_solution(16260141445112365050)
XLA Ops:
  6.5 0.7 all-gather.6.cloned.1.call-update
  7.3 0.0 all-gather.4.cloned.1.call-start
  7.3 0.7 all-gather.4.cloned.1.call-update
  8.0 0.0 all-gather.8.cloned.1.call-start
  8.1 0.1 pad.2.clone
  8.1 0.1 pad.3.clone
  8.2 0.7 fusion.7
  9.0 57.4 %all-gather.6.cloned.1.call-done = bf16[512,8192]{1,0:T(8,128)(2,1)} async-done(((bf16[512,1024]{1,0:T(8,128)(2,1)}), bf16[512,8192]{1,0:T(8,128)(2,1)}) %all-gather.6.cloned.1.call-update) | async-done | bytes 8388624 | tf_op jit(solution)/shard_map/all_gather | solution.py:120
  66.4 10.3 %convert_multiply_fusion = (f32[512,512]{1,0:T(8,128)S(1)}, bf16[512,512]{1,0:T(8,128)(2,1)S(1)}) fusion(bf16[512,512]{1,0:T(8,128)(2,1)} %param.11, bf16[512,8192]{1,0:T(8,128)(2,1)} %all-gather.6.cloned.1.call-done, bf16[512,8192]{1,0:T(8,128)(2,1)} %param.13), kind=kOutput, calls=%fused_computation.4 | convolution fusion | flops 4296015872 | bytes 18874368 | tf_op jit(solution)/shard_map/dot_general | solution.py:119
  76.7 0.0 copy-start.1
  76.7 0.0 copy-start.2
  76.7 0.4 reshape.51
  77.1 0.6 reduce_sum.30
  77.8 0.1 copy.101
  77.9 0.1 concatenate.10
  78.0 0.1 copy.95
  78.2 1.0 maximum_maximum_fusion
  79.2 0.0 all-gather.8.cloned.1.call-update
  79.3 14.3 %all_gather.15 = s32[4,2048,4]{1,2,0:T(4,128)S(1)} all-gather(s32[4,512,4]{1,2,0:T(4,128)S(1)} %copy-done.1), channel_id=1, replica_groups=mesh['grp'=4,'pb'=8] {'grp'}, dimensions={1}, use_global_device_ids=true | all-gather | bytes 163840 | tf_op jit(solution)/shard_map/all_gather | solution.py:112
  93.6 0.2 select_reduce_fusion
  93.8 0.2 compare_reduce_fusion
  94.0 0.2 fusion
  94.2 0.2 copy.96
  94.4 0.3 reshape_reshape.3
  94.7 0.4 reshape.54.rows
  95.0 0.0 copy-start
  95.1 8.6 %copy.98 = s32[4,4,2,2048]{2,3,1,0:T(8,128)} copy(s32[4,4,2,2048]{3,2,1,0:T(2,128)S(1)} %reshape_reshape.3) | data formatting | bytes 524288 | tf_op jit(solution)/shard_map/reshape;reshape | solution.py:117
  103.7 12.3 %all-gather.4.cloned.1.call-done.q = bf16[2048,512]{1,0:T(8,128)(2,1)} async-done(((bf16[512,512]{1,0:T(8,128)(2,1)}), bf16[2048,512]{1,0:T(8,128)(2,1)}) %all-gather.4.cloned.1.call-update) | async-done | bytes 2097168 | tf_op jit(solution)/shard_map/all_gather | solution.py:113
  116.0 55.2 %all-gather.8.cloned.1.call-done.g.aux = bf16[2048,640]{1,0:T(8,128)(2,1)} async-done(((bf16[512,640]{1,0:T(8,128)(2,1)}), bf16[2048,640]{1,0:T(8,128)(2,1)}) %all-gather.8.cloned.1.call-update) | async-done | bytes 2621456 | tf_op jit(solution)/shard_map/all_gather | solution.py:134
  171.2 54.2 %shard_map.100 = bf16[2048,512]{1,0:T(8,128)(2,1)S(1)} custom-call(s32[4,8]{1,0:T(4,128)S(1)} %copy-done, bf16[2048,512]{1,0:T(8,128)(2,1)} %all-gather.4.cloned.1.call-done.q, bf16[2048,640]{1,0:T(8,128)(2,1)} %all-gather.8.cloned.1.call-done.g.aux, bf16[2048,640]{1,0:T(8,128)(2,1)} %all-gather.8.cloned.1.call-done.g.aux, ...), custom_call_target="tpu_custom_call" | custom-call | tf_op jit(solution)/shard_map/pallas_call | solution.py:136
  225.3 50.9 %all_to_all.5 = bf16[4,512,512]{2,1,0:T(8,128)(2,1)S(1)} all-to-all(bf16[4,512,512]{2,1,0:T(8,128)(2,1)S(1)} %bitcast.26), channel_id=1, replica_groups=mesh['grp'=4,'pb'=8] {'grp'}, dimensions={0} | all-to-all | bytes 4194304 | tf_op jit(solution)/shard_map/all_to_all | solution.py:154
  276.2 1.2 reduce_sum.32
  (15 shorter events, 0.1 us)
Async XLA Ops:
  6.5 59.9 %all-gather.6.cloned.1.call-start = ((), (), s32[]{:S(2)}) async-start(), calls=%async_computation.2 | async-start | bytes 9437184 | tf_op jit(solution)/shard_map/all_gather | solution.py:120
  7.3 108.7 %all-gather.4.cloned.1.call-start = ((), (), s32[]{:S(2)}) async-start(), calls=%async_computation.1 | async-start | bytes 2621440 | tf_op jit(solution)/shard_map/all_gather | solution.py:113
  8.0 163.1 %all-gather.8.cloned.1.call-start = ((), (), s32[]{:S(2)}) async-start(), calls=%async_computation.3 | async-start | bytes 3276800 | tf_op jit(solution)/shard_map/all_gather | solution.py:134
  76.7 2.5 copy-start.1
  76.7 16.8 %copy-start.2 = (s32[4,32]{1,0:T(4,128)S(1)}, s32[4,32]{1,0:T(4,128)}, u32[]{:S(2)}) copy-start(s32[4,32]{1,0:T(4,128)} %param.16) | copy-start | bytes 1540
  95.0 76.1 %copy-start = (s32[4,8]{1,0:T(4,128)S(1)}, s32[4,8]{1,0:T(4,128)}, u32[]{:S(2)}) copy-start(s32[4,8]{1,0:T(4,128)} %counts.1) | copy-start | bytes 388
Sparse Core Ops, SparseCore 0:
  9.3 57.0 all-gather.5
  68.0 47.9 all-gather.3
  117.5 53.5 all-gather.7

commit v2 on v1

--- a/solution.py
+++ b/solution.py
@@ -10,6 +10,8 @@
 LANES = 128
 AUX = 8
 PAIR = 2
+CHUNKS = 4
+MESH = pl.DeviceIdType.MESH
 
 
 def three_parts(x):
@@ -37,6 +39,208 @@
         preferred_element_type=jnp.float32,
     )
     return jnp.where(marked, before.astype(jnp.int32), -1)
+
+
+def readout_kernel(
+    groups, heads, width, r, w, outputs, base, full, rbuf, wbuf, rsend, rrecv, zsend, zrecv, local_sem, wsem
+):
+    p, z = lax.axis_index("pb"), lax.axis_index("grp")
+    token_count, depth = r.shape
+    blocks = rbuf.shape[0]
+    chunk = token_count // CHUNKS
+    half = chunk // 2
+
+    def flip(bit, q):
+        return q + bit - 2 * bit * lax.rem(lax.div(q, bit), 2)
+
+    core, across, along = flip(1, p), flip(2, p), flip(4, p)
+    corner = flip(4, across)
+    has_left, has_right = z > 0, z < groups - 1
+    neighbours = jnp.where(has_left, 1, 0) + jnp.where(has_right, 1, 0)
+
+    barrier = pltpu.get_barrier_semaphore()
+    for other in (core, across, along):
+        pl.semaphore_signal(barrier, inc=1, device_id={"pb": other}, device_id_type=MESH)
+
+    @pl.when(has_left)
+    def _():
+        pl.semaphore_signal(barrier, inc=1, device_id={"grp": z - 1}, device_id_type=MESH)
+
+    @pl.when(has_right)
+    def _():
+        pl.semaphore_signal(barrier, inc=1, device_id={"grp": z + 1}, device_id_type=MESH)
+
+    own_block = pltpu.make_async_copy(r, rbuf.at[p], local_sem)
+    own_block.start()
+    weights = [
+        pltpu.make_async_copy(w.at[:, pl.ds(b * depth, depth)], wbuf.at[b], wsem.at[b]) for b in range(blocks)
+    ]
+    for copy in weights:
+        copy.start()
+    pl.semaphore_wait(barrier, 3 + neighbours)
+
+    def hop(kind, t, block, target, own=False):
+        first = t * chunk + (half if kind in (6, 8) else 0)
+        where = pl.ds(first, half if kind in (5, 6, 7, 8) else chunk)
+        return pltpu.make_async_remote_copy(
+            src_ref=r.at[where] if own else rbuf.at[block, where],
+            dst_ref=rbuf.at[block, where],
+            send_sem=rsend.at[t, kind],
+            recv_sem=rrecv.at[t, kind],
+            device_id={"pb": target},
+            device_id_type=MESH,
+        )
+
+    started = []
+
+    def start(*what, **kw):
+        copy = hop(*what, **kw)
+        copy.start()
+        started.append(copy)
+
+    def send_own(t):
+        start(1, t, p, across, own=True)
+        start(2, t, p, along, own=True)
+        start(0, t, p, core, own=True)
+
+    def zhop(t, source, way):
+        where = full.at[source, pl.ds(t * chunk, chunk)]
+        return pltpu.make_async_remote_copy(
+            src_ref=where,
+            dst_ref=where,
+            send_sem=zsend.at[t, source, (way + 1) // 2],
+            recv_sem=zrecv.at[t, source],
+            device_id={"grp": z + way},
+            device_id_type=MESH,
+        )
+
+    def pass_on(t, distance):
+        for way in (1, -1):
+            source = z - way * distance
+            here = (source >= 0) & (source < groups)
+            onward = (z + way >= 0) & (z + way < groups)
+
+            @pl.when(here)
+            def _():
+                zhop(t, source, way).wait_recv()
+
+            @pl.when(here & onward)
+            def _():
+                zhop(t, source, way).start()
+
+    def finish(t, distance):
+        for way in (1, -1):
+            source = z - way * distance
+
+            @pl.when((source >= 0) & (source < groups) & (z + way >= 0) & (z + way < groups))
+            def _():
+                zhop(t, source, way).wait_send()
+
+    def multiply(t):
+        rows = pl.ds(t * chunk, chunk)
+        total = jnp.zeros((chunk, wbuf.shape[1]), jnp.float32)
+        for b in range(blocks):
+            total += lax.dot_general(
+                rbuf[b, rows, :], wbuf[b], (((1,), (1,)), ((), ())), preferred_element_type=jnp.float32
+            )
+        grad = total.astype(jnp.bfloat16)
+        product = grad.astype(jnp.float32) * outputs[rows, :].astype(jnp.float32)
+        lane = lax.broadcasted_iota(jnp.int32, (chunk, LANES), 1)
+        aux = base[rows, :]
+        for h in range(heads):
+            delta = -jnp.sum(product[:, h * width : (h + 1) * width], axis=1, keepdims=True)
+            high = delta.astype(jnp.bfloat16).astype(jnp.float32)
+            rest = delta - high
+            middle = rest.astype(jnp.bfloat16).astype(jnp.float32)
+            for i, part in enumerate((high, middle, rest - middle)):
+                aux = jnp.where(lane == h * AUX + 3 + i, part, aux)
+        full[z, rows, : heads * width] = grad
+        full[z, rows, heads * width :] = aux.astype(jnp.bfloat16)
+
+    send_own(0)
+    send_own(1)
+    own_block.wait()
+    for t in range(CHUNKS + groups - 1):
+        if t < CHUNKS:
+            hop(1, t, across, across).wait_recv()
+            start(5, t, across, along)
+            start(3, t, across, core)
+            hop(2, t, along, along).wait_recv()
+            start(6, t, along, across)
+            start(4, t, along, core)
+            if t + 2 < CHUNKS:
+                send_own(t + 2)
+        if 1 <= t <= CHUNKS:
+            last = t - 1
+            hop(5, last, corner, along).wait_recv()
+            start(7, last, corner, core)
+            hop(6, last, corner, across).wait_recv()
+            start(8, last, corner, core)
+        for distance in range(1, groups - 1):
+            if 0 <= t - 1 - distance < CHUNKS:
+                pass_on(t - 1 - distance, distance)
+        if 1 <= t <= CHUNKS:
+            if t == 1:
+                for copy in weights:
+                    copy.wait()
+            hop(0, last, core, core).wait_recv()
+            hop(3, last, flip(2, core), core).wait_recv()
+            hop(4, last, flip(4, core), core).wait_recv()
+            hop(7, last, flip(1, corner), core).wait_recv()
+            hop(8, last, flip(1, corner), core).wait_recv()
+            multiply(last)
+
+            @pl.when(has_right)
+            def _():
+                zhop(last, z, 1).start()
+
+            @pl.when(has_left)
+            def _():
+                zhop(last, z, -1).start()
+
+    for t in range(CHUNKS):
+        for way in (1, -1):
+            source = z - way * (groups - 1)
+
+            @pl.when((source >= 0) & (source < groups))
+            def _():
+                zhop(t, source, way).wait_recv()
+
+    for copy in started:
+        copy.wait_send()
+    for t in range(CHUNKS):
+        for distance in range(groups - 1):
+            finish(t, distance)
+
+
+def readout(readout_grad, readout_weight, outputs, base, groups, heads, width):
+    token_count, depth = readout_grad.shape
+    features = readout_weight.shape[0]
+    blocks = lax.axis_size("pb")
+    columns = features + LANES
+    vmem = pl.BlockSpec(memory_space=pltpu.VMEM)
+    return pl.pallas_call(
+        functools.partial(readout_kernel, groups, heads, width),
+        in_specs=[vmem, pl.BlockSpec(memory_space=pl.ANY), vmem, vmem],
+        out_specs=vmem,
+        out_shape=jax.ShapeDtypeStruct((groups, token_count, columns), jnp.bfloat16),
+        scratch_shapes=[
+            pltpu.VMEM((blocks, token_count, depth), jnp.bfloat16),
+            pltpu.VMEM((blocks, features, depth), jnp.bfloat16),
+            pltpu.SemaphoreType.DMA((CHUNKS, 9)),
+            pltpu.SemaphoreType.DMA((CHUNKS, 9)),
+            pltpu.SemaphoreType.DMA((CHUNKS, groups, 2)),
+            pltpu.SemaphoreType.DMA((CHUNKS, groups)),
+            pltpu.SemaphoreType.DMA,
+            pltpu.SemaphoreType.DMA((blocks,)),
+        ],
+        compiler_params=pltpu.CompilerParams(
+            collective_id=0, has_side_effects=True, vmem_limit_bytes=50 * 2**20
+        ),
+        cost_estimate=pl.CostEstimate(
+            flops=2 * token_count * features * depth * blocks, bytes_accessed=32 * 2**20, transcendentals=0
+        ),
+    )(readout_grad, readout_weight, outputs, base)
 
 
 def grad_kernel(groups, capacity, scale, counts, q, g, aux, rows, cols, keys, values, out, total):
@@ -109,29 +313,41 @@
     scale = width ** (-0.5)
     every = groups * token_count
 
-    all_probes = lax.all_gather(probes, "grp", axis=1, tiled=True)
-    all_queries = lax.all_gather(queries, "grp", axis=0, tiled=True)
+    steps = local_clusters // PAIR
+    probe_lanes = probes.transpose(1, 0, 2).reshape(token_count, heads * probes.shape[2])
+    probe_lanes = jnp.pad(probe_lanes, ((0, 0), (0, LANES - probe_lanes.shape[1]))).astype(jnp.bfloat16)
+    all_queries = lax.all_gather(jnp.concatenate([queries, probe_lanes], axis=1), "grp", axis=0, tiled=True)
+    base = jnp.concatenate(
+        [three_parts(log_norm * (-1.0 / scale)), jnp.zeros((token_count, heads, AUX - 3))], axis=2
+    ).reshape(token_count, heads * AUX)
+    base = jnp.concatenate(
+        [base, jnp.zeros((token_count, LANES - 1 - heads * AUX)), jnp.ones((token_count, 1))], axis=1
+    )
+
+    if groups == 4 and lax.axis_size("pb") == 8:
+        all_grads = readout(readout_grad, readout_weight, outputs, base, groups, heads, width)
+        all_grads = all_grads.reshape(every, heads * width + LANES)
+    else:
+        grad_out = lax.dot_general(
+            lax.all_gather(readout_grad, "pb", axis=1, tiled=True),
+            readout_weight,
+            (((1,), (1,)), ((), ())),
+            preferred_element_type=jnp.float32,
+        ).astype(jnp.bfloat16)
+        row_delta = jnp.sum(
+            (grad_out.astype(jnp.float32) * outputs.astype(jnp.float32)).reshape(token_count, heads, width), axis=2
+        )
+        deltas = jnp.pad(three_parts(-row_delta), ((0, 0), (0, 0), (3, AUX - 6))).reshape(token_count, heads * AUX)
+        aux = base + jnp.pad(deltas, ((0, 0), (0, LANES - heads * AUX)))
+        all_grads = lax.all_gather(
+            jnp.concatenate([grad_out, aux.astype(jnp.bfloat16)], axis=1), "grp", axis=0, tiled=True
+        )
+
+    all_probes = all_queries[:, heads * width : heads * width + heads * probes.shape[2]].astype(jnp.int32)
+    all_probes = all_probes.reshape(every, heads, probes.shape[2]).transpose(1, 0, 2)
     ranks = probe_ranks(all_probes, owner_slots, local_clusters, token_count, groups)
     ranks = ranks.reshape(heads, local_clusters, 1, every)
-    steps = local_clusters // PAIR
     rank_cols = ranks.reshape(heads, steps, PAIR, every).transpose(0, 1, 3, 2)
-
-    grad_out = lax.dot_general(
-        lax.all_gather(readout_grad, "pb", axis=1, tiled=True),
-        readout_weight,
-        (((1,), (1,)), ((), ())),
-        preferred_element_type=jnp.float32,
-    ).astype(jnp.bfloat16)
-    row_delta = jnp.sum(
-        (grad_out.astype(jnp.float32) * outputs.astype(jnp.float32)).reshape(token_count, heads, width), axis=2
-    )
-    aux = jnp.concatenate(
-        [three_parts(log_norm * (-1.0 / scale)), three_parts(-row_delta), jnp.zeros((token_count, heads, 2))], axis=2
-    ).reshape(token_count, heads * AUX)
-    aux = jnp.concatenate(
-        [aux, jnp.zeros((token_count, LANES - 1 - heads * AUX)), jnp.ones((token_count, 1))], axis=1
-    ).astype(jnp.bfloat16)
-    all_grads = lax.all_gather(jnp.concatenate([grad_out, aux], axis=1), "grp", axis=0, tiled=True)
 
     partial = pl.pallas_call(
         functools.partial(grad_kernel, groups, capacity, scale),

time: 284 us -> 237 us (0.83)
  waiting for transfers between devices: 126 us -> 0.04 us
  Pallas kernels: 54.2 us -> 155 us
  blocking collectives: 65.2 us -> 50.9 us
  matrix products: 10.6 us -> 0.25 us
    all_gather x3 -> x1, waiting for transfers between devices: 125 us -> 0.02 us  [shards(): lax.all_gather(jnp.concatenate([queries, probe_lanes], axis=1), 'grp', ax...]
    pallas_call x0 -> x1, Pallas kernels: none -> 101 us  [readout(): pl.pallas_call(functools.partial(readout_kernel, groups, heads, width), i...]
    all_gather x1 -> x0, blocking collectives: 14.3 us -> none  [shards(): all_probes = lax.all_gather(probes, 'grp', axis=1, tiled=True)]
    dot_general x1 -> x0, matrix products: 10.3 us -> none  [shards(): lax.dot_general(lax.all_gather(readout_grad, 'pb', axis=1, tiled=True), r...]
  transfers between devices with their start and end apart: 3 -> 1, of which waited for: 3 -> 0; matrix products, arithmetic and copies ran while one was open for 8% -> 1% of each run, Pallas kernels for 0% -> 43%
where the time goes in v2:
time: 237 us; the launch traced here: 236 us
  Pallas kernels  155 us (65%)
  blocking collectives  50.9 us (21%)
  between operations  13.6 us (6%)
  local copies, waits for them, and re-layouts  10.3 us (4%)
  other arithmetic  6.44 us (3%)
    pallas_call x1, Pallas kernels, readout(): pl.pallas_call(functools.partial(readout_kernel, groups, heads, width), i...  101 us
    pallas_call x1, Pallas kernels, shards(): pl.pallas_call(functools.partial(grad_kernel, groups, capacity, scale), g...  54.1 us
    all_to_all x1, blocking collectives, shards(): lax.all_to_all(partial.reshape(groups, token_count, heads * width), 'grp'...  50.9 us
    another operation x2, local copies, waits for them, and re-layouts, shards(): rank_cols = ranks.reshape(heads, steps, PAIR, every).transpose(0, 1, 3, 2)  8.93 us
  transfers between devices with their start and end apart: 1, of which 0 were waited for; matrix products, arithmetic and copies ran while one was open for 1% of the time, Pallas kernels for 43%

profile of v2, /device:TPU:0, one launch (start us, length us, event | category | flops | bytes accessed | tf_op | source)
XLA Modules:
  0.0 236.5 jit_solution(5214825865411559501)
XLA Ops:
  6.5 0.0 copy-start.3
  6.5 0.0 copy-start.2
  6.5 0.0 all-gather.2.cloned.1.call-start
  6.5 0.9 convert_bitcast_fusion
  7.4 0.1 copy.34
  7.6 1.9 fusion.4
  9.5 0.0 all-gather.2.cloned.1.call-update
  9.5 0.1 pad.7.clone
  9.6 0.1 pad.12.clone
  9.7 0.1 pad.8.clone
  9.8 0.7 reduce-precision_bitcast_fusion.1
  10.5 0.1 maximum_bitcast_fusion
  10.6 0.1 copy.37
  10.7 0.0 copy-done.3
  10.8 0.2 select_reduce_fusion
  11.0 0.0 copy-done.1
  11.0 0.0 copy-done.2
  11.0 100.8 %shard_map.100 = bf16[4,512,640]{2,1,0:T(8,128)(2,1)} custom-call(bf16[512,1024]{1,0:T(8,128)(2,1)S(1)} %copy-done.1, bf16[512,8192]{1,0:T(8,128)(2,1)} %w.1, bf16[512,512]{1,0:T(8,128)(2,1)S(1)} %copy-done.2, f32[512,128]{1,0:T(8,128)S(1)} %maximum_maximum_fusion.base), custom_call_target="tpu_custom_call" | custom-call | flops 4294967296 | bytes 33554432 | tf_op jit(solution)/shard_map/pallas_call | solution.py:222
  111.9 0.0 all-gather.2.cloned.1.call-done.q
  111.9 1.1 slice_convert_fusion
  113.1 0.3 copy.38
  113.4 0.2 compare_reduce_fusion
  113.6 0.2 fusion.1
  113.9 0.2 copy.39
  114.1 0.3 reshape_reshape.3
  114.3 0.4 reshape.35.rows
  114.7 0.0 copy-start
  114.7 8.7 %copy.41 = s32[4,4,2,2048]{2,3,1,0:T(8,128)} copy(s32[4,4,2,2048]{3,2,1,0:T(2,128)S(1)} %reshape_reshape.3) | data formatting | bytes 524288 | tf_op jit(solution)/shard_map/reshape;reshape | solution.py:350
  123.4 0.0 copy-done
  123.4 54.1 %shard_map.101 = bf16[2048,512]{1,0:T(8,128)(2,1)S(1)} custom-call(s32[4,8]{1,0:T(4,128)S(1)} %copy-done, bf16[2048,640]{1,0:T(8,128)(2,1)} %all-gather.2.cloned.1.call-done.q, bf16[2048,640]{1,0:T(8,128)(2,1)} %bitcast.28, bf16[2048,640]{1,0:T(8,128)(2,1)} %bitcast.29, s32[4,8,1,2048]{3,2,1,0:T(1,128)S(1)} %reshape.35.rows, s32[4,4,2048,2]{3,2,1,0:T(8,128)} %bitcast.27, ...), custom_call_target="tpu_custom_call" | custom-call | tf_op jit(solution)/shard_map/pallas_call | solution.py:352
  177.5 50.9 %all_to_all.5 = bf16[4,512,512]{2,1,0:T(8,128)(2,1)S(1)} all-to-all(bf16[4,512,512]{2,1,0:T(8,128)(2,1)S(1)} %bitcast.26), channel_id=1, replica_groups=mesh['grp'=4,'pb'=8] {'grp'}, dimensions={0} | all-to-all | bytes 4194304 | tf_op jit(solution)/shard_map/all_to_all | solution.py:370
  228.4 1.2 reduce_sum.22
  (10 shorter events, 0.1 us)
Async XLA Ops:
  6.5 4.2 %copy-start.3 = (s32[4,32]{1,0:T(4,128)S(1)}, s32[4,32]{1,0:T(4,128)}, u32[]{:S(2)}) copy-start(s32[4,32]{1,0:T(4,128)} %param.16) | copy-start | bytes 1540
  6.5 4.5 %copy-start.1 = (bf16[512,1024]{1,0:T(8,128)(2,1)S(1)}, bf16[512,1024]{1,0:T(8,128)(2,1)}, u32[]{:S(2)}) copy-start(bf16[512,1024]{1,0:T(8,128)(2,1)} %r.1) | copy-start | bytes 3145732
  6.5 4.5 %copy-start.2 = (bf16[512,512]{1,0:T(8,128)(2,1)S(1)}, bf16[512,512]{1,0:T(8,128)(2,1)}, u32[]{:S(2)}) copy-start(bf16[512,512]{1,0:T(8,128)(2,1)} %outputs.1) | copy-start | bytes 1572868
  6.5 105.4 %all-gather.2.cloned.1.call-start = ((), (), s32[]{:S(2)}) async-start(), calls=%async_computation.1 | async-start | bytes 3276800 | tf_op jit(solution)/shard_map/all_gather | solution.py:319
  114.7 8.7 %copy-start = (s32[4,8]{1,0:T(4,128)S(1)}, s32[4,8]{1,0:T(4,128)}, u32[]{:S(2)}) copy-start(s32[4,8]{1,0:T(4,128)} %counts.1) | copy-start | bytes 388
Sparse Core Ops, SparseCore 0:
  9.7 70.1 all-gather.1

commit v3 on v2

--- a/solution.py
+++ b/solution.py
@@ -21,14 +21,14 @@
     return jnp.stack([high, middle, rest - middle], axis=-1)
 
 
-def probe_ranks(probes, owner_slots, local_clusters, token_count, groups):
-    me = lax.axis_index("grp")
-    clusters = owner_slots.shape[1]
-    cluster_ids = jnp.arange(clusters, dtype=jnp.int32)
-    slots = me * local_clusters + jnp.arange(local_clusters, dtype=jnp.int32)
-    named = jnp.sum(
-        jnp.where(owner_slots[:, None, :] == slots[None, :, None], cluster_ids, 0), axis=2, dtype=jnp.int32
-    )
+def named_clusters(owner_slots, local_clusters):
+    cluster_ids = jnp.arange(owner_slots.shape[1], dtype=jnp.int32)
+    slots = lax.axis_index("grp") * local_clusters + jnp.arange(local_clusters, dtype=jnp.int32)
+    return jnp.sum(jnp.where(owner_slots[:, None, :] == slots[None, :, None], cluster_ids, 0), axis=2, dtype=jnp.int32)
+
+
+def probe_ranks(probes, named, token_count, groups):
+    local_clusters = named.shape[1]
     marked = jnp.any(probes[:, None, :, :] == named[:, :, None, None], axis=3)
     marked = marked.reshape(probes.shape[0], local_clusters, groups, token_count)
     earlier = jnp.arange(token_count)[:, None] < jnp.arange(token_count)[None, :]
@@ -42,7 +42,8 @@
 
 
 def readout_kernel(
-    groups, heads, width, r, w, outputs, base, full, rbuf, wbuf, rsend, rrecv, zsend, zrecv, local_sem, wsem
+    groups, heads, width, r, w, outputs, base, q, probes, named, full, qall, rows_out, cols_out, rbuf, wbuf, pbuf,
+    rsend, rrecv, zsend, zrecv, local_sem, wsem
 ):
     p, z = lax.axis_index("pb"), lax.axis_index("grp")
     token_count, depth = r.shape
@@ -104,7 +105,12 @@
         start(0, t, p, core, own=True)
 
     def zhop(t, source, way):
-        where = full.at[source, pl.ds(t * chunk, chunk)]
+        if t < CHUNKS:
+            where = full.at[source, pl.ds(t * chunk, chunk)]
+        elif t < 2 * CHUNKS:
+            where = qall.at[source, pl.ds((t - CHUNKS) * chunk, chunk)]
+        else:
+            where = pbuf.at[source]
         return pltpu.make_async_remote_copy(
             src_ref=where,
             dst_ref=where,
@@ -157,7 +163,51 @@
         full[z, rows, : heads * width] = grad
         full[z, rows, heads * width :] = aux.astype(jnp.bfloat16)
 
+    def zsend_own(t):
+        @pl.when(has_right)
+        def _():
+            zhop(t, z, 1).start()
+
+        @pl.when(has_left)
+        def _():
+            zhop(t, z, -1).start()
+
+    def zlast(t):
+        for way in (1, -1):
+            source = z - way * (groups - 1)
+
+            @pl.when((source >= 0) & (source < groups))
+            def _():
+                zhop(t, source, way).wait_recv()
+
+    def rank():
+        earlier = lax.broadcasted_iota(jnp.int32, (token_count, token_count), 0) < lax.broadcasted_iota(
+            jnp.int32, (token_count, token_count), 1
+        )
+        earlier = earlier.astype(jnp.bfloat16)
+        local = named.shape[0] // heads
+        count = pbuf.shape[1] // heads
+        for group in range(groups):
+            marked = []
+            for h in range(heads):
+                ids = named[h * local : (h + 1) * local, :]
+                hit = jnp.zeros((local, token_count), jnp.float32)
+                for j in range(count):
+                    at = h * count + j
+                    hit += jnp.where(pbuf[group, at : at + 1, :] == ids, 1.0, 0.0)
+                marked.append(hit)
+            marked = jnp.concatenate(marked, axis=0)
+            before = jnp.dot(marked.astype(jnp.bfloat16), earlier, preferred_element_type=jnp.float32)
+            ranks = jnp.where(marked > 0.5, before, -1.0)
+            rows_out[group] = ranks.astype(jnp.int32)
+            padded = jnp.concatenate([ranks, jnp.zeros((LANES - ranks.shape[0], token_count), jnp.float32)], axis=0)
+            cols_out[group] = padded.T.astype(jnp.int32)
+
+    qall[z] = q[...]
+    pbuf[z] = probes[...]
     send_own(0)
+    for t in (2 * CHUNKS, *range(CHUNKS, 2 * CHUNKS)):
+        zsend_own(t)
     send_own(1)
     own_block.wait()
     for t in range(CHUNKS + groups - 1):
@@ -176,6 +226,9 @@
             start(7, last, corner, core)
             hop(6, last, corner, across).wait_recv()
             start(8, last, corner, core)
+        early = {0: [8, 4, 5, 6], 1: [7, 8, 4, 5, 6], 2: [7]}.get(t, [])
+        for k, piece in enumerate(early):
+            pass_on(piece, 1 if t == 0 or (t == 1 and k == 0) else 2)
         for distance in range(1, groups - 1):
             if 0 <= t - 1 - distance < CHUNKS:
                 pass_on(t - 1 - distance, distance)
@@ -189,48 +242,45 @@
             hop(7, last, flip(1, corner), core).wait_recv()
             hop(8, last, flip(1, corner), core).wait_recv()
             multiply(last)
-
-            @pl.when(has_right)
-            def _():
-                zhop(last, z, 1).start()
-
-            @pl.when(has_left)
-            def _():
-                zhop(last, z, -1).start()
-
-    for t in range(CHUNKS):
-        for way in (1, -1):
-            source = z - way * (groups - 1)
-
-            @pl.when((source >= 0) & (source < groups))
-            def _():
-                zhop(t, source, way).wait_recv()
+            zsend_own(last)
+        if t == 2:
+            zlast(2 * CHUNKS)
+            rank()
+
+    for t in range(2 * CHUNKS):
+        zlast(t)
 
     for copy in started:
         copy.wait_send()
-    for t in range(CHUNKS):
+    for t in range(2 * CHUNKS + 1):
         for distance in range(groups - 1):
             finish(t, distance)
 
 
-def readout(readout_grad, readout_weight, outputs, base, groups, heads, width):
+def readout(readout_grad, readout_weight, outputs, base, queries, probes, named, groups, heads, width):
     token_count, depth = readout_grad.shape
     features = readout_weight.shape[0]
     blocks = lax.axis_size("pb")
-    columns = features + LANES
     vmem = pl.BlockSpec(memory_space=pltpu.VMEM)
+    pieces = 2 * CHUNKS + 1
     return pl.pallas_call(
         functools.partial(readout_kernel, groups, heads, width),
-        in_specs=[vmem, pl.BlockSpec(memory_space=pl.ANY), vmem, vmem],
-        out_specs=vmem,
-        out_shape=jax.ShapeDtypeStruct((groups, token_count, columns), jnp.bfloat16),
+        in_specs=[vmem, pl.BlockSpec(memory_space=pl.ANY), vmem, vmem, vmem, vmem, vmem],
+        out_specs=[vmem] * 4,
+        out_shape=[
+            jax.ShapeDtypeStruct((groups, token_count, features + LANES), jnp.bfloat16),
+            jax.ShapeDtypeStruct((groups, token_count, features), jnp.bfloat16),
+            jax.ShapeDtypeStruct((groups, named.shape[0], token_count), jnp.int32),
+            jax.ShapeDtypeStruct((groups, token_count, LANES), jnp.int32),
+        ],
         scratch_shapes=[
             pltpu.VMEM((blocks, token_count, depth), jnp.bfloat16),
             pltpu.VMEM((blocks, features, depth), jnp.bfloat16),
+            pltpu.VMEM((groups,) + probes.shape, jnp.int32),
             pltpu.SemaphoreType.DMA((CHUNKS, 9)),
             pltpu.SemaphoreType.DMA((CHUNKS, 9)),
-            pltpu.SemaphoreType.DMA((CHUNKS, groups, 2)),
-            pltpu.SemaphoreType.DMA((CHUNKS, groups)),
+            pltpu.SemaphoreType.DMA((pieces, groups, 2)),
+            pltpu.SemaphoreType.DMA((pieces, groups)),
             pltpu.SemaphoreType.DMA,
             pltpu.SemaphoreType.DMA((blocks,)),
         ],
@@ -240,7 +290,138 @@
         cost_estimate=pl.CostEstimate(
             flops=2 * token_count * features * depth * blocks, bytes_accessed=32 * 2**20, transcendentals=0
         ),
-    )(readout_grad, readout_weight, outputs, base)
+    )(readout_grad, readout_weight, outputs, base, queries, probes, named)
+
+
+def attend_kernel(
+    groups, capacity, scale, counts, q, g, rows, cols, keys, values, out,
+    kbuf, vbuf, turned, partials, outgoing, arrived, ksem, vsem, ssem, rsem
+):
+    me = lax.axis_index("grp")
+    heads, local, span, width = kbuf.shape
+    token_count = q.shape[1]
+    contract_last = (((1,), (1,)), ((), ()))
+
+    barrier = pltpu.get_barrier_semaphore()
+    for d in range(1, groups):
+        pl.semaphore_signal(
+            barrier, inc=1, device_id={"grp": lax.rem(me + d, groups)}, device_id_type=MESH
+        )
+
+    def loads(h):
+        return (
+            pltpu.make_async_copy(keys.at[h], kbuf.at[h], ksem.at[h]),
+            pltpu.make_async_copy(values.at[h], vbuf.at[h], vsem.at[h]),
+        )
+
+    def home(h, d):
+        there = lax.rem(me + d, groups)
+        return pltpu.make_async_remote_copy(
+            src_ref=outgoing.at[h, there],
+            dst_ref=arrived.at[h, d - 1],
+            send_sem=ssem.at[h, d - 1],
+            recv_sem=rsem.at[h, d - 1],
+            device_id={"grp": there},
+            device_id_type=MESH,
+        )
+
+    for h in range(heads):
+        for copy in loads(h):
+            copy.start()
+    pl.semaphore_wait(barrier, groups - 1)
+
+    lane = lax.broadcasted_iota(jnp.int32, (span, LANES), 1)
+    key_id = lax.broadcasted_iota(jnp.int32, (span, LANES), 0)
+    place = lax.broadcasted_iota(jnp.int32, (capacity, token_count), 0)
+    spot = lax.broadcasted_iota(jnp.int32, (token_count, capacity), 1)
+
+    def one_head(h, carry):
+        for copy in loads(h):
+            copy.wait()
+        own = lane - h * AUX
+        ones = jnp.where((own >= 0) & (own < 3), 1.0, 0.0)
+        value_side = jnp.where((own >= 3) & (own < 6), 1.0, 0.0).astype(jnp.bfloat16)
+        columns = pl.ds(pl.multiple_of(h * width, width), width)
+        aux_at = heads * width
+        for c in range(local):
+            valid = counts[h, c]
+            key_side = jnp.where((lane == LANES - 1) & (key_id >= valid), -1e30, ones).astype(jnp.bfloat16)
+            picked = []
+            for group in range(groups):
+                chosen = (rows[group, pl.ds(h * local + c, 1), :] == place).astype(jnp.bfloat16)
+                rhs = jnp.concatenate(
+                    [q[group, :, columns], g[group, :, aux_at : aux_at + LANES], g[group, :, columns]], axis=1
+                )
+                picked.append(jnp.dot(chosen, rhs, preferred_element_type=jnp.float32).astype(jnp.bfloat16))
+            picked = jnp.concatenate(picked, axis=0)
+            key_block, value_block = kbuf[h, c], vbuf[h, c]
+            scores = lax.dot_general(
+                picked[:, : 2 * LANES],
+                jnp.concatenate([key_block, key_side], axis=1),
+                contract_last,
+                preferred_element_type=jnp.float32,
+            )
+            grad_prob = lax.dot_general(
+                picked[:, LANES:],
+                jnp.concatenate([value_side, value_block], axis=1),
+                contract_last,
+                preferred_element_type=jnp.float32,
+            )
+            grad_score = (jnp.exp(scores * scale) * grad_prob).astype(jnp.bfloat16)
+            part = jnp.dot(grad_score, key_block, preferred_element_type=jnp.float32).astype(jnp.bfloat16)
+            for group in range(groups):
+                partials[group, c * capacity : (c + 1) * capacity, :] = part[
+                    group * capacity : (group + 1) * capacity
+                ]
+        for group in range(groups):
+            turned[...] = pltpu.roll(cols[group], lax.rem(LANES - h * local, LANES), 1)
+            chosen = jnp.concatenate(
+                [(turned[:, c : c + 1] == spot).astype(jnp.bfloat16) for c in range(local)], axis=1
+            )
+            total = jnp.dot(chosen, partials[group], preferred_element_type=jnp.float32)
+            outgoing[h, group] = (total * scale).astype(jnp.bfloat16)
+        for d in range(1, groups):
+            home(h, d).start()
+        return carry
+
+    lax.fori_loop(0, heads, one_head, 0)
+    for h in range(heads):
+        total = outgoing[h, me].astype(jnp.float32)
+        for d in range(1, groups):
+            home(h, d).wait_recv()
+            total += arrived[h, d - 1].astype(jnp.float32)
+        out[:, h * width : (h + 1) * width] = total.astype(out.dtype)
+    for h in range(heads):
+        for d in range(1, groups):
+            home(h, d).wait_send()
+
+
+def attend(counts, q, g, rows, cols, keys, values, capacity, scale):
+    groups, token_count, features = q.shape
+    heads, local, span, width = keys.shape
+    vmem = pl.BlockSpec(memory_space=pltpu.VMEM)
+    hbm = pl.BlockSpec(memory_space=pl.ANY)
+    return pl.pallas_call(
+        functools.partial(attend_kernel, groups, capacity, scale),
+        in_specs=[pl.BlockSpec(memory_space=pltpu.SMEM), vmem, vmem, vmem, vmem, hbm, hbm],
+        out_specs=vmem,
+        out_shape=jax.ShapeDtypeStruct((token_count, features), jnp.bfloat16),
+        scratch_shapes=[
+            pltpu.VMEM(keys.shape, jnp.bfloat16),
+            pltpu.VMEM(values.shape, jnp.bfloat16),
+            pltpu.VMEM((token_count, LANES), jnp.int32),
+            pltpu.VMEM((groups, local * capacity, width), jnp.bfloat16),
+            pltpu.VMEM((heads, groups, token_count, width), jnp.bfloat16),
+            pltpu.VMEM((heads, groups - 1, token_count, width), jnp.bfloat16),
+            pltpu.SemaphoreType.DMA((heads,)),
+            pltpu.SemaphoreType.DMA((heads,)),
+            pltpu.SemaphoreType.DMA((heads, groups - 1)),
+            pltpu.SemaphoreType.DMA((heads, groups - 1)),
+        ],
+        compiler_params=pltpu.CompilerParams(
+            collective_id=1, has_side_effects=True, vmem_limit_bytes=50 * 2**20
+        ),
+    )(counts, q, g, rows, cols, keys, values)
 
 
 def grad_kernel(groups, capacity, scale, counts, q, g, aux, rows, cols, keys, values, out, total):
@@ -314,9 +495,7 @@
     every = groups * token_count
 
     steps = local_clusters // PAIR
-    probe_lanes = probes.transpose(1, 0, 2).reshape(token_count, heads * probes.shape[2])
-    probe_lanes = jnp.pad(probe_lanes, ((0, 0), (0, LANES - probe_lanes.shape[1]))).astype(jnp.bfloat16)
-    all_queries = lax.all_gather(jnp.concatenate([queries, probe_lanes], axis=1), "grp", axis=0, tiled=True)
+    named = named_clusters(owner_slots, local_clusters)
     base = jnp.concatenate(
         [three_parts(log_norm * (-1.0 / scale)), jnp.zeros((token_count, heads, AUX - 3))], axis=2
     ).reshape(token_count, heads * AUX)
@@ -325,27 +504,41 @@
     )
 
     if groups == 4 and lax.axis_size("pb") == 8:
-        all_grads = readout(readout_grad, readout_weight, outputs, base, groups, heads, width)
-        all_grads = all_grads.reshape(every, heads * width + LANES)
-    else:
-        grad_out = lax.dot_general(
-            lax.all_gather(readout_grad, "pb", axis=1, tiled=True),
+        all_grads, all_queries, rows, cols = readout(
+            readout_grad,
             readout_weight,
-            (((1,), (1,)), ((), ())),
-            preferred_element_type=jnp.float32,
-        ).astype(jnp.bfloat16)
-        row_delta = jnp.sum(
-            (grad_out.astype(jnp.float32) * outputs.astype(jnp.float32)).reshape(token_count, heads, width), axis=2
-        )
-        deltas = jnp.pad(three_parts(-row_delta), ((0, 0), (0, 0), (3, AUX - 6))).reshape(token_count, heads * AUX)
-        aux = base + jnp.pad(deltas, ((0, 0), (0, LANES - heads * AUX)))
-        all_grads = lax.all_gather(
-            jnp.concatenate([grad_out, aux.astype(jnp.bfloat16)], axis=1), "grp", axis=0, tiled=True
-        )
+            outputs,
+            base,
+            queries,
+            probes.transpose(0, 2, 1).reshape(heads * probes.shape[2], token_count),
+            named.reshape(heads * local_clusters, 1),
+            groups,
+            heads,
+            width,
+        )
+        return attend(counts, all_queries, all_grads, rows, cols, cluster_keys, values, capacity, scale)
+
+    probe_lanes = probes.transpose(1, 0, 2).reshape(token_count, heads * probes.shape[2])
+    probe_lanes = jnp.pad(probe_lanes, ((0, 0), (0, LANES - probe_lanes.shape[1]))).astype(jnp.bfloat16)
+    all_queries = lax.all_gather(jnp.concatenate([queries, probe_lanes], axis=1), "grp", axis=0, tiled=True)
+    grad_out = lax.dot_general(
+        lax.all_gather(readout_grad, "pb", axis=1, tiled=True),
+        readout_weight,
+        (((1,), (1,)), ((), ())),
+        preferred_element_type=jnp.float32,
+    ).astype(jnp.bfloat16)
+    row_delta = jnp.sum(
+        (grad_out.astype(jnp.float32) * outputs.astype(jnp.float32)).reshape(token_count, heads, width), axis=2
+    )
+    deltas = jnp.pad(three_parts(-row_delta), ((0, 0), (0, 0), (3, AUX - 6))).reshape(token_count, heads * AUX)
+    aux = base + jnp.pad(deltas, ((0, 0), (0, LANES - heads * AUX)))
+    all_grads = lax.all_gather(
+        jnp.concatenate([grad_out, aux.astype(jnp.bfloat16)], axis=1), "grp", axis=0, tiled=True
+    )
 
     all_probes = all_queries[:, heads * width : heads * width + heads * probes.shape[2]].astype(jnp.int32)
     all_probes = all_probes.reshape(every, heads, probes.shape[2]).transpose(1, 0, 2)
-    ranks = probe_ranks(all_probes, owner_slots, local_clusters, token_count, groups)
+    ranks = probe_ranks(all_probes, named, token_count, groups)
     ranks = ranks.reshape(heads, local_clusters, 1, every)
     rank_cols = ranks.reshape(heads, steps, PAIR, every).transpose(0, 1, 3, 2)
 

time: 237 us -> 152 us (0.64)
  blocking collectives: 50.9 us -> 0 us
  between operations: 13.6 us -> 0.09 us
  Pallas kernels: 155 us -> 143 us
  other arithmetic: 6.44 us -> 1.72 us
  local copies, waits for them, and re-layouts: 10.3 us -> 6.92 us
    all_to_all x1 -> x0, blocking collectives: 50.9 us -> none  [shards(): lax.all_to_all(partial.reshape(groups, token_count, heads * width), 'grp'...]
    pallas_call x1, Pallas kernels: 101 us -> 86.9 us  [readout(): pl.pallas_call(functools.partial(readout_kernel, groups, heads, width), i...]
    another operation x2 -> x0, local copies, waits for them, and re-layouts: 8.93 us -> none  [shards(): rank_cols = ranks.reshape(heads, steps, PAIR, every).transpose(0, 1, 3, 2)]
    unnamed x8 -> x11, local copies, waits for them, and re-layouts: 0.02 us -> 5.69 us
  transfers between devices with their start and end apart: 1 -> 0, of which waited for: 0 -> 0; matrix products, arithmetic and copies ran while one was open for 1% -> 0% of each run, Pallas kernels for 43% -> 0%
where the time goes in v3:
time: 152 us
  Pallas kernels  143 us (94%)
  local copies, waits for them, and re-layouts  6.92 us (5%)
  other arithmetic  1.72 us (1%)
    pallas_call x1, Pallas kernels, readout(): pl.pallas_call(functools.partial(readout_kernel, groups, heads, width), i...  86.9 us
    pallas_call x1, Pallas kernels, attend(): pl.pallas_call(functools.partial(attend_kernel, groups, capacity, scale),...  55.9 us
    unnamed x11, local copies, waits for them, and re-layouts  5.69 us

profile of v3, /device:TPU:0, one launch (start us, length us, event | category | flops | bytes accessed | tf_op | source)
XLA Modules:
  0.0 151.5 jit_solution(7837268707241155355)
XLA Ops:
  0.0 0.1 pad.1.clone
  0.1 0.1 pad.6.clone
  0.2 0.1 pad.2.clone
  0.2 0.9 select_reduce_fusion
  1.1 0.1 reshape.17.named
  1.2 0.7 reduce-precision_bitcast_fusion.1
  2.0 0.8 reshape.15.probes
  2.7 0.1 maximum_bitcast_fusion
  2.8 0.1 copy.21
  3.0 0.0 copy-start.2
  3.0 1.2 copy-done.2
  4.2 0.0 copy-start.3
  4.2 1.0 copy-done.3
  5.3 0.0 copy-start.4
  5.3 1.0 copy-done.4
  6.3 0.0 copy-start.1
  6.3 86.9 %shard_map.100 = (bf16[4,512,640]{2,1,0:T(8,128)(2,1)}, bf16[4,512,512]{2,1,0:T(8,128)(2,1)}, s32[4,32,512]{2,1,0:T(8,128)S(1)}, s32[4,512,128]{2,1,0:T(8,128)S(1)}) custom-call(bf16[512,1024]{1,0:T(8,128)(2,1)S(1)} %copy-done.2, bf16[512,8192]{1,0:T(8,128)(2,1)} %w.1, bf16[512,512]{1,0:T(8,128)(2,1)S(1)} %copy-done.3, ...), custom_call_target="tpu_custom_call" | custom-call | flops 4294967296 | bytes 33554432 | tf_op jit(solution)/shard_map/pallas_call | solution.py:266
  93.2 0.0 copy-done.1
  93.2 0.0 copy-start
  93.3 1.6 %copy-done = bf16[4,512,512]{2,1,0:T(8,128)(2,1)S(1)} copy-done((bf16[4,512,512]{2,1,0:T(8,128)(2,1)S(1)}, bf16[4,512,512]{2,1,0:T(8,128)(2,1)}, u32[]{:S(2)}) %copy-start) | copy-done | bytes 2097176
  94.8 55.9 %shard_map.101 = bf16[512,512]{1,0:T(8,128)(2,1)S(1)} custom-call(s32[4,8]{1,0:T(4,128)S(1)} %copy-done.1, bf16[4,512,512]{2,1,0:T(8,128)(2,1)S(1)} %copy-done, bf16[4,512,640]{2,1,0:T(8,128)(2,1)} %get-tuple-element.10.g, s32[4,32,512]{2,1,0:T(8,128)S(1)} %get-tuple-element.11.rows, s32[4,512,128]{2,1,0:T(8,128)S(1)} %get-tuple-element.12.cols, ...), custom_call_target="tpu_custom_call" | custom-call | tf_op jit(solution)/shard_map/pallas_call | solution.py:404
  150.7 0.8 copy.24
  (7 shorter events, 0.1 us)
Async XLA Ops:
  3.0 1.2 copy-start.2
  4.2 1.0 copy-start.3
  5.3 1.0 copy-start.4
  6.3 86.9 %copy-start.1 = (s32[4,8]{1,0:T(4,128)S(1)}, s32[4,8]{1,0:T(4,128)}, u32[]{:S(2)}) copy-start(s32[4,8]{1,0:T(4,128)} %counts.1) | copy-start | bytes 388
  93.2 1.6 %copy-start = (bf16[4,512,512]{2,1,0:T(8,128)(2,1)S(1)}, bf16[4,512,512]{2,1,0:T(8,128)(2,1)}, u32[]{:S(2)}) copy-start(bf16[4,512,512]{2,1,0:T(8,128)(2,1)} %get-tuple-element.9.q) | copy-start | bytes 6291460

commit v4 on v3

--- a/solution.py
+++ b/solution.py
@@ -12,6 +12,7 @@
 PAIR = 2
 CHUNKS = 4
 MESH = pl.DeviceIdType.MESH
+PASSES = {0: ((4, 1), (0, 1), (1, 1)), 1: ((2, 1), (3, 1), (4, 2), (0, 2)), 2: ((1, 2), (2, 2), (3, 2))}
 
 
 def three_parts(x):
@@ -41,8 +42,54 @@
     return jnp.where(marked, before.astype(jnp.int32), -1)
 
 
+def line(groups, z, place, zsend, zrecv):
+    def hop(piece, source, way):
+        where = place(piece, source)
+        return pltpu.make_async_remote_copy(
+            src_ref=where,
+            dst_ref=where,
+            send_sem=zsend.at[piece, source, (way + 1) // 2],
+            recv_sem=zrecv.at[piece, source],
+            device_id={"grp": z + way},
+            device_id_type=MESH,
+        )
+
+    def inside(q):
+        return (q >= 0) & (q < groups)
+
+    def send_own(piece):
+        for way in (1, -1):
+
+            @pl.when(inside(z + way))
+            def _():
+                hop(piece, z, way).start()
+
+    def pass_on(piece, distance):
+        for way in (1, -1):
+            source = z - way * distance
+
+            @pl.when(inside(source))
+            def _():
+                hop(piece, source, way).wait_recv()
+
+            @pl.when(inside(source) & inside(z + way))
+            def _():
+                hop(piece, source, way).start()
+
+    def finish(piece):
+        for distance in range(groups - 1):
+            for way in (1, -1):
+                source = z - way * distance
+
+                @pl.when(inside(source) & inside(z + way))
+                def _():
+                    hop(piece, source, way).wait_send()
+
+    return send_own, pass_on, finish
+
+
 def readout_kernel(
-    groups, heads, width, r, w, outputs, base, q, probes, named, full, qall, rows_out, cols_out, rbuf, wbuf, pbuf,
+    groups, heads, width, r, w, outputs, base, q, probes, named, grads, aux_rows, qall, rows_out, cols_out, rbuf, wbuf, pbuf,
     rsend, rrecv, zsend, zrecv, local_sem, wsem
 ):
     p, z = lax.axis_index("pb"), lax.axis_index("grp")
@@ -104,43 +151,12 @@
         start(2, t, p, along, own=True)
         start(0, t, p, core, own=True)
 
-    def zhop(t, source, way):
-        if t < CHUNKS:
-            where = full.at[source, pl.ds(t * chunk, chunk)]
-        elif t < 2 * CHUNKS:
-            where = qall.at[source, pl.ds((t - CHUNKS) * chunk, chunk)]
-        else:
-            where = pbuf.at[source]
-        return pltpu.make_async_remote_copy(
-            src_ref=where,
-            dst_ref=where,
-            send_sem=zsend.at[t, source, (way + 1) // 2],
-            recv_sem=zrecv.at[t, source],
-            device_id={"grp": z + way},
-            device_id_type=MESH,
-        )
-
-    def pass_on(t, distance):
-        for way in (1, -1):
-            source = z - way * distance
-            here = (source >= 0) & (source < groups)
-            onward = (z + way >= 0) & (z + way < groups)
-
-            @pl.when(here)
-            def _():
-                zhop(t, source, way).wait_recv()
-
-            @pl.when(here & onward)
-            def _():
-                zhop(t, source, way).start()
-
-    def finish(t, distance):
-        for way in (1, -1):
-            source = z - way * distance
-
-            @pl.when((source >= 0) & (source < groups) & (z + way >= 0) & (z + way < groups))
-            def _():
-                zhop(t, source, way).wait_send()
+    def place(piece, source):
+        if piece < CHUNKS:
+            return qall.at[source, pl.ds(piece * chunk, chunk)]
+        return pbuf.at[source]
+
+    zsend_own, pass_on, finish = line(groups, z, place, zsend, zrecv)
 
     def multiply(t):
         rows = pl.ds(t * chunk, chunk)
@@ -160,25 +176,8 @@
             middle = rest.astype(jnp.bfloat16).astype(jnp.float32)
             for i, part in enumerate((high, middle, rest - middle)):
                 aux = jnp.where(lane == h * AUX + 3 + i, part, aux)
-        full[z, rows, : heads * width] = grad
-        full[z, rows, heads * width :] = aux.astype(jnp.bfloat16)
-
-    def zsend_own(t):
-        @pl.when(has_right)
-        def _():
-            zhop(t, z, 1).start()
-
-        @pl.when(has_left)
-        def _():
-            zhop(t, z, -1).start()
-
-    def zlast(t):
-        for way in (1, -1):
-            source = z - way * (groups - 1)
-
-            @pl.when((source >= 0) & (source < groups))
-            def _():
-                zhop(t, source, way).wait_recv()
+        grads[rows, :] = grad
+        aux_rows[:, rows] = aux.T[: heads * AUX].astype(jnp.bfloat16)
 
     def rank():
         earlier = lax.broadcasted_iota(jnp.int32, (token_count, token_count), 0) < lax.broadcasted_iota(
@@ -206,11 +205,11 @@
     qall[z] = q[...]
     pbuf[z] = probes[...]
     send_own(0)
-    for t in (2 * CHUNKS, *range(CHUNKS, 2 * CHUNKS)):
-        zsend_own(t)
+    for piece in (CHUNKS, *range(CHUNKS)):
+        zsend_own(piece)
     send_own(1)
     own_block.wait()
-    for t in range(CHUNKS + groups - 1):
+    for t in range(CHUNKS + 1):
         if t < CHUNKS:
             hop(1, t, across, across).wait_recv()
             start(5, t, across, along)
@@ -226,12 +225,8 @@
             start(7, last, corner, core)
             hop(6, last, corner, across).wait_recv()
             start(8, last, corner, core)
-        early = {0: [8, 4, 5, 6], 1: [7, 8, 4, 5, 6], 2: [7]}.get(t, [])
-        for k, piece in enumerate(early):
-            pass_on(piece, 1 if t == 0 or (t == 1 and k == 0) else 2)
-        for distance in range(1, groups - 1):
-            if 0 <= t - 1 - distance < CHUNKS:
-                pass_on(t - 1 - distance, distance)
+        for piece, distance in PASSES.get(t, ()):
+            pass_on(piece, distance)
         if 1 <= t <= CHUNKS:
             if t == 1:
                 for copy in weights:
@@ -242,19 +237,16 @@
             hop(7, last, flip(1, corner), core).wait_recv()
             hop(8, last, flip(1, corner), core).wait_recv()
             multiply(last)
-            zsend_own(last)
-        if t == 2:
-            zlast(2 * CHUNKS)
+        if t == CHUNKS - 1:
+            pass_on(CHUNKS, groups - 1)
             rank()
 
-    for t in range(2 * CHUNKS):
-        zlast(t)
-
+    for piece in range(CHUNKS):
+        pass_on(piece, groups - 1)
     for copy in started:
         copy.wait_send()
-    for t in range(2 * CHUNKS + 1):
-        for distance in range(groups - 1):
-            finish(t, distance)
+    for piece in range(CHUNKS + 1):
+        finish(piece)
 
 
 def readout(readout_grad, readout_weight, outputs, base, queries, probes, named, groups, heads, width):
@@ -262,13 +254,14 @@
     features = readout_weight.shape[0]
     blocks = lax.axis_size("pb")
     vmem = pl.BlockSpec(memory_space=pltpu.VMEM)
-    pieces = 2 * CHUNKS + 1
+    pieces = CHUNKS + 1
     return pl.pallas_call(
         functools.partial(readout_kernel, groups, heads, width),
         in_specs=[vmem, pl.BlockSpec(memory_space=pl.ANY), vmem, vmem, vmem, vmem, vmem],
-        out_specs=[vmem] * 4,
+        out_specs=[vmem] * 5,
         out_shape=[
-            jax.ShapeDtypeStruct((groups, token_count, features + LANES), jnp.bfloat16),
+            jax.ShapeDtypeStruct((token_count, features), jnp.bfloat16),
+            jax.ShapeDtypeStruct((heads * AUX, token_count), jnp.bfloat16),
             jax.ShapeDtypeStruct((groups, token_count, features), jnp.bfloat16),
             jax.ShapeDtypeStruct((groups, named.shape[0], token_count), jnp.int32),
             jax.ShapeDtypeStruct((groups, token_count, LANES), jnp.int32),
@@ -294,8 +287,8 @@
 
 
 def attend_kernel(
-    groups, capacity, scale, counts, q, g, rows, cols, keys, values, out,
-    kbuf, vbuf, turned, partials, outgoing, arrived, ksem, vsem, ssem, rsem
+    groups, capacity, scale, counts, q, grads, aux_rows, rows, cols, keys, values, out,
+    kbuf, vbuf, g, tbuf, aux, turned, partials, outgoing, arrived, ksem, vsem, ssem, rsem, zsend, zrecv
 ):
     me = lax.axis_index("grp")
     heads, local, span, width = kbuf.shape
@@ -325,32 +318,58 @@
             device_id_type=MESH,
         )
 
+    def spot_of(piece, source):
+        if isinstance(piece, int) and piece == heads:
+            return tbuf.at[source]
+        return g.at[source, piece]
+
+    send_own, pass_on, finish = line(groups, me, spot_of, zsend, zrecv)
+
+    tbuf[me] = aux_rows[...]
+    for h in range(heads):
+        g[me, h] = grads[:, h * width : (h + 1) * width]
+    pl.semaphore_wait(barrier, groups - 1)
+    send_own(heads)
+    send_own(0)
+    send_own(1)
     for h in range(heads):
         for copy in loads(h):
             copy.start()
-    pl.semaphore_wait(barrier, groups - 1)
+    pass_on(heads, 1)
+    pass_on(0, 1)
+    send_own(2)
+    pass_on(heads, 2)
+    pass_on(0, 2)
+    send_own(3)
+    pass_on(1, 1)
+    pass_on(heads, groups - 1)
+    for group in range(groups):
+        wide = tbuf[group].astype(jnp.float32)
+        wide = jnp.concatenate([wide, jnp.zeros((LANES - wide.shape[0], token_count), jnp.float32)], axis=0)
+        aux[group] = wide.T.astype(jnp.bfloat16)
+    later = [(1, 2), (2, 1), (2, 2), (3, 1), (3, 2)]
 
     lane = lax.broadcasted_iota(jnp.int32, (span, LANES), 1)
     key_id = lax.broadcasted_iota(jnp.int32, (span, LANES), 0)
     place = lax.broadcasted_iota(jnp.int32, (capacity, token_count), 0)
     spot = lax.broadcasted_iota(jnp.int32, (token_count, capacity), 1)
 
-    def one_head(h, carry):
+    def one_head(h, later):
         for copy in loads(h):
             copy.wait()
+        pass_on(h, groups - 1)
         own = lane - h * AUX
         ones = jnp.where((own >= 0) & (own < 3), 1.0, 0.0)
         value_side = jnp.where((own >= 3) & (own < 6), 1.0, 0.0).astype(jnp.bfloat16)
         columns = pl.ds(pl.multiple_of(h * width, width), width)
-        aux_at = heads * width
         for c in range(local):
             valid = counts[h, c]
-            key_side = jnp.where((lane == LANES - 1) & (key_id >= valid), -1e30, ones).astype(jnp.bfloat16)
+            key_side = jnp.where((lane == AUX - 1) & (key_id >= valid), -1e30, ones).astype(jnp.bfloat16)
             picked = []
             for group in range(groups):
                 chosen = (rows[group, pl.ds(h * local + c, 1), :] == place).astype(jnp.bfloat16)
                 rhs = jnp.concatenate(
-                    [q[group, :, columns], g[group, :, aux_at : aux_at + LANES], g[group, :, columns]], axis=1
+                    [q[group, :, columns], aux[group], g[group, h]], axis=1
                 )
                 picked.append(jnp.dot(chosen, rhs, preferred_element_type=jnp.float32).astype(jnp.bfloat16))
             picked = jnp.concatenate(picked, axis=0)
@@ -373,6 +392,8 @@
                 partials[group, c * capacity : (c + 1) * capacity, :] = part[
                     group * capacity : (group + 1) * capacity
                 ]
+            if c < len(later):
+                pass_on(*later[c])
         for group in range(groups):
             turned[...] = pltpu.roll(cols[group], lax.rem(LANES - h * local, LANES), 1)
             chosen = jnp.concatenate(
@@ -382,9 +403,14 @@
             outgoing[h, group] = (total * scale).astype(jnp.bfloat16)
         for d in range(1, groups):
             home(h, d).start()
+
+    one_head(0, later)
+
+    def next_head(h, carry):
+        one_head(h, ())
         return carry
 
-    lax.fori_loop(0, heads, one_head, 0)
+    lax.fori_loop(1, heads, next_head, 0)
     for h in range(heads):
         total = outgoing[h, me].astype(jnp.float32)
         for d in range(1, groups):
@@ -394,21 +420,26 @@
     for h in range(heads):
         for d in range(1, groups):
             home(h, d).wait_send()
-
-
-def attend(counts, q, g, rows, cols, keys, values, capacity, scale):
+    for piece in range(heads + 1):
+        finish(piece)
+
+
+def attend(counts, q, grads, aux_rows, rows, cols, keys, values, capacity, scale):
     groups, token_count, features = q.shape
     heads, local, span, width = keys.shape
     vmem = pl.BlockSpec(memory_space=pltpu.VMEM)
     hbm = pl.BlockSpec(memory_space=pl.ANY)
     return pl.pallas_call(
         functools.partial(attend_kernel, groups, capacity, scale),
-        in_specs=[pl.BlockSpec(memory_space=pltpu.SMEM), vmem, vmem, vmem, vmem, hbm, hbm],
+        in_specs=[pl.BlockSpec(memory_space=pltpu.SMEM), vmem, vmem, vmem, vmem, vmem, hbm, hbm],
         out_specs=vmem,
         out_shape=jax.ShapeDtypeStruct((token_count, features), jnp.bfloat16),
         scratch_shapes=[
             pltpu.VMEM(keys.shape, jnp.bfloat16),
             pltpu.VMEM(values.shape, jnp.bfloat16),
+            pltpu.VMEM((groups, heads, token_count, width), jnp.bfloat16),
+            pltpu.VMEM((groups,) + aux_rows.shape, jnp.bfloat16),
+            pltpu.VMEM((groups, token_count, LANES), jnp.bfloat16),
             pltpu.VMEM((token_count, LANES), jnp.int32),
             pltpu.VMEM((groups, local * capacity, width), jnp.bfloat16),
             pltpu.VMEM((heads, groups, token_count, width), jnp.bfloat16),
@@ -417,11 +448,13 @@
             pltpu.SemaphoreType.DMA((heads,)),
             pltpu.SemaphoreType.DMA((heads, groups - 1)),
             pltpu.SemaphoreType.DMA((heads, groups - 1)),
+            pltpu.SemaphoreType.DMA((heads + 1, groups, 2)),
+            pltpu.SemaphoreType.DMA((heads + 1, groups)),
         ],
         compiler_params=pltpu.CompilerParams(
             collective_id=1, has_side_effects=True, vmem_limit_bytes=50 * 2**20
         ),
-    )(counts, q, g, rows, cols, keys, values)
+    )(counts, q, grads, aux_rows, rows, cols, keys, values)
 
 
 def grad_kernel(groups, capacity, scale, counts, q, g, aux, rows, cols, keys, values, out, total):
@@ -438,7 +471,7 @@
     partials = []
     for i in range(PAIR):
         valid = counts[head, step * PAIR + i]
-        key_side = jnp.where((lane == LANES - 1) & (key_id >= valid), -1e30, ones).astype(jnp.bfloat16)
+        key_side = jnp.where((lane == AUX - 1) & (key_id >= valid), -1e30, ones).astype(jnp.bfloat16)
         key_block, value_block = keys[0, i], values[0, i]
         picked = []
         for group in range(groups):
@@ -497,14 +530,17 @@
     steps = local_clusters // PAIR
     named = named_clusters(owner_slots, local_clusters)
     base = jnp.concatenate(
-        [three_parts(log_norm * (-1.0 / scale)), jnp.zeros((token_count, heads, AUX - 3))], axis=2
+        [
+            three_parts(log_norm * (-1.0 / scale)),
+            jnp.zeros((token_count, heads, AUX - 4)),
+            jnp.ones((token_count, heads, 1)),
+        ],
+        axis=2,
     ).reshape(token_count, heads * AUX)
-    base = jnp.concatenate(
-        [base, jnp.zeros((token_count, LANES - 1 - heads * AUX)), jnp.ones((token_count, 1))], axis=1
-    )
-
-    if groups == 4 and lax.axis_size("pb") == 8:
-        all_grads, all_queries, rows, cols = readout(
+    base = jnp.pad(base, ((0, 0), (0, LANES - heads * AUX)))
+
+    if groups == 4 and heads == 4 and lax.axis_size("pb") == 8:
+        grads, aux_rows, all_queries, rows, cols = readout(
             readout_grad,
             readout_weight,
             outputs,
@@ -516,7 +552,7 @@
             heads,
             width,
         )
-        return attend(counts, all_queries, all_grads, rows, cols, cluster_keys, values, capacity, scale)
+        return attend(counts, all_queries, grads, aux_rows, rows, cols, cluster_keys, values, capacity, scale)
 
     probe_lanes = probes.transpose(1, 0, 2).reshape(token_count, heads * probes.shape[2])
     probe_lanes = jnp.pad(probe_lanes, ((0, 0), (0, LANES - probe_lanes.shape[1]))).astype(jnp.bfloat16)

time: 152 us -> 139 us (0.914)
  Pallas kernels: 143 us -> 133 us
  local copies, waits for them, and re-layouts: 6.92 us -> 3.99 us
    pallas_call x1, Pallas kernels: 86.9 us -> 49.6 us  [readout(): pl.pallas_call(functools.partial(readout_kernel, groups, heads, width), i...]
    pallas_call x1, Pallas kernels: 55.9 us -> 83.2 us  [attend(): pl.pallas_call(functools.partial(attend_kernel, groups, capacity, scale),...]
    unnamed x11 -> x7, local copies, waits for them, and re-layouts: 5.69 us -> 2.88 us
where the time goes in v4:
time: 139 us; the launch traced here: 138 us
  Pallas kernels  133 us (96%)
  local copies, waits for them, and re-layouts  3.99 us (3%)
  other arithmetic  1.61 us (1%)
    pallas_call x1, Pallas kernels, attend(): pl.pallas_call(functools.partial(attend_kernel, groups, capacity, scale),...  83.2 us
    pallas_call x1, Pallas kernels, readout(): pl.pallas_call(functools.partial(readout_kernel, groups, heads, width), i...  49.6 us
    unnamed x7, local copies, waits for them, and re-layouts  2.88 us

profile of v4, /device:TPU:0, one launch (start us, length us, event | category | flops | bytes accessed | tf_op | source)
XLA Modules:
  0.0 138.4 jit_solution(2715441469862953484)
XLA Ops:
  0.0 0.9 select_reduce_fusion
  0.9 0.1 reshape.17.named
  1.0 0.7 reduce-precision_subtract_fusion
  1.7 0.8 reshape.15.probes
  2.5 0.1 concatenate.3
  2.6 0.1 copy.21
  2.8 0.0 copy-start.1
  2.8 1.0 copy-done.1
  3.8 0.0 copy-start.2
  3.8 1.0 copy-done.2
  4.9 0.0 copy-start
  4.9 49.6 %shard_map.100 = (bf16[512,512]{1,0:T(8,128)(2,1)S(1)}, bf16[32,512]{1,0:T(8,128)(2,1)S(1)}, bf16[4,512,512]{2,1,0:T(8,128)(2,1)}, s32[4,32,512]{2,1,0:T(8,128)S(1)}, s32[4,512,128]{2,1,0:T(8,128)S(1)}) custom-call(bf16[512,1024]{1,0:T(8,128)(2,1)} %r.1, bf16[512,8192]{1,0:T(8,128)(2,1)} %w.1, bf16[512,512]{1,0:T(8,128)(2,1)S(1)} %copy-done.1, ...), custom_call_target="tpu_custom_call" | custom-call | flops 4294967296 | bytes 33554432 | tf_op jit(solution)/shard_map/pallas_call | solution.py:258
  54.5 0.0 copy-done
  54.5 83.2 %shard_map.101 = bf16[512,512]{1,0:T(8,128)(2,1)S(1)} custom-call(s32[4,8]{1,0:T(4,128)S(1)} %copy-done, bf16[4,512,512]{2,1,0:T(8,128)(2,1)} %get-tuple-element.10.q, bf16[512,512]{1,0:T(8,128)(2,1)S(1)} %get-tuple-element.11.grads, bf16[32,512]{1,0:T(8,128)(2,1)S(1)} %get-tuple-element.12.aux_rows, s32[4,32,512]{2,1,0:T(8,128)S(1)} %get-tuple-element.13.rows, ...), custom_call_target="tpu_custom_call" | custom-call | tf_op jit(solution)/shard_map/pallas_call | solution.py:432
  137.6 0.8 copy.24
  (7 shorter events, 0.1 us)
Async XLA Ops:
  2.8 1.0 copy-start.1
  3.8 1.0 copy-start.2
  4.9 49.6 %copy-start = (s32[4,8]{1,0:T(4,128)S(1)}, s32[4,8]{1,0:T(4,128)}, u32[]{:S(2)}) copy-start(s32[4,8]{1,0:T(4,128)} %counts.1) | copy-start | bytes 388

commit v5 on v4

--- a/solution.py
+++ b/solution.py
@@ -11,8 +11,9 @@
 AUX = 8
 PAIR = 2
 CHUNKS = 4
+EARLY = 2
 MESH = pl.DeviceIdType.MESH
-PASSES = {0: ((4, 1), (0, 1), (1, 1)), 1: ((2, 1), (3, 1), (4, 2), (0, 2)), 2: ((1, 2), (2, 2), (3, 2))}
+PASSES = {0: ((4, 1), (0, 1), (1, 1)), 1: ((2, 1), (3, 1), (4, 2), (0, 2)), 2: ((1, 2), (2, 2), (3, 2)), 3: ((5, 1),), 4: ((5, 2), (6, 1))}
 
 
 def three_parts(x):
@@ -89,7 +90,7 @@
 
 
 def readout_kernel(
-    groups, heads, width, r, w, outputs, base, q, probes, named, grads, aux_rows, qall, rows_out, cols_out, rbuf, wbuf, pbuf,
+    groups, heads, width, r, w, outputs, base, q, probes, named, grads, first, aux_rows, qall, rows_out, cols_out, rbuf, wbuf, pbuf,
     rsend, rrecv, zsend, zrecv, local_sem, wsem
 ):
     p, z = lax.axis_index("pb"), lax.axis_index("grp")
@@ -154,7 +155,9 @@
     def place(piece, source):
         if piece < CHUNKS:
             return qall.at[source, pl.ds(piece * chunk, chunk)]
-        return pbuf.at[source]
+        if piece == CHUNKS:
+            return pbuf.at[source]
+        return first.at[source, pl.ds((piece - CHUNKS - 1) * chunk, chunk)]
 
     zsend_own, pass_on, finish = line(groups, z, place, zsend, zrecv)
 
@@ -176,7 +179,10 @@
             middle = rest.astype(jnp.bfloat16).astype(jnp.float32)
             for i, part in enumerate((high, middle, rest - middle)):
                 aux = jnp.where(lane == h * AUX + 3 + i, part, aux)
-        grads[rows, :] = grad
+        if t < EARLY:
+            first[z, rows, :] = grad
+        else:
+            grads[pl.ds((t - EARLY) * chunk, chunk), :] = grad
         aux_rows[:, rows] = aux.T[: heads * AUX].astype(jnp.bfloat16)
 
     def rank():
@@ -237,15 +243,18 @@
             hop(7, last, flip(1, corner), core).wait_recv()
             hop(8, last, flip(1, corner), core).wait_recv()
             multiply(last)
+            if last < EARLY:
+                zsend_own(CHUNKS + 1 + last)
         if t == CHUNKS - 1:
             pass_on(CHUNKS, groups - 1)
             rank()
 
-    for piece in range(CHUNKS):
+    pass_on(CHUNKS + EARLY, 2)
+    for piece in (*range(CHUNKS), *range(CHUNKS + 1, CHUNKS + 1 + EARLY)):
         pass_on(piece, groups - 1)
     for copy in started:
         copy.wait_send()
-    for piece in range(CHUNKS + 1):
+    for piece in range(CHUNKS + 1 + EARLY):
         finish(piece)
 
 
@@ -254,13 +263,15 @@
     features = readout_weight.shape[0]
     blocks = lax.axis_size("pb")
     vmem = pl.BlockSpec(memory_space=pltpu.VMEM)
-    pieces = CHUNKS + 1
+    pieces = CHUNKS + 1 + EARLY
+    early = token_count // CHUNKS * EARLY
     return pl.pallas_call(
         functools.partial(readout_kernel, groups, heads, width),
         in_specs=[vmem, pl.BlockSpec(memory_space=pl.ANY), vmem, vmem, vmem, vmem, vmem],
-        out_specs=[vmem] * 5,
+        out_specs=[vmem] * 6,
         out_shape=[
-            jax.ShapeDtypeStruct((token_count, features), jnp.bfloat16),
+            jax.ShapeDtypeStruct((token_count - early, features), jnp.bfloat16),
+            jax.ShapeDtypeStruct((groups, early, features), jnp.bfloat16),
             jax.ShapeDtypeStruct((heads * AUX, token_count), jnp.bfloat16),
             jax.ShapeDtypeStruct((groups, token_count, features), jnp.bfloat16),
             jax.ShapeDtypeStruct((groups, named.shape[0], token_count), jnp.int32),
@@ -287,7 +298,7 @@
 
 
 def attend_kernel(
-    groups, capacity, scale, counts, q, grads, aux_rows, rows, cols, keys, values, out,
+    groups, capacity, scale, counts, q, grads, first, aux_rows, rows, cols, keys, values, out,
     kbuf, vbuf, g, tbuf, aux, turned, partials, outgoing, arrived, ksem, vsem, ssem, rsem, zsend, zrecv
 ):
     me = lax.axis_index("grp")
@@ -321,13 +332,14 @@
     def spot_of(piece, source):
         if isinstance(piece, int) and piece == heads:
             return tbuf.at[source]
-        return g.at[source, piece]
-
+        return g.at[source, piece, pl.ds(early, token_count - early)]
+
+    early = first.shape[1]
     send_own, pass_on, finish = line(groups, me, spot_of, zsend, zrecv)
 
     tbuf[me] = aux_rows[...]
     for h in range(heads):
-        g[me, h] = grads[:, h * width : (h + 1) * width]
+        g[me, h, early:, :] = grads[:, h * width : (h + 1) * width]
     pl.semaphore_wait(barrier, groups - 1)
     send_own(heads)
     send_own(0)
@@ -335,6 +347,9 @@
     for h in range(heads):
         for copy in loads(h):
             copy.start()
+    for group in range(groups):
+        for h in range(heads):
+            g[group, h, :early, :] = first[group, :, h * width : (h + 1) * width]
     pass_on(heads, 1)
     pass_on(0, 1)
     send_own(2)
@@ -424,14 +439,14 @@
         finish(piece)
 
 
-def attend(counts, q, grads, aux_rows, rows, cols, keys, values, capacity, scale):
+def attend(counts, q, grads, first, aux_rows, rows, cols, keys, values, capacity, scale):
     groups, token_count, features = q.shape
     heads, local, span, width = keys.shape
     vmem = pl.BlockSpec(memory_space=pltpu.VMEM)
     hbm = pl.BlockSpec(memory_space=pl.ANY)
     return pl.pallas_call(
         functools.partial(attend_kernel, groups, capacity, scale),
-        in_specs=[pl.BlockSpec(memory_space=pltpu.SMEM), vmem, vmem, vmem, vmem, vmem, hbm, hbm],
+        in_specs=[pl.BlockSpec(memory_space=pltpu.SMEM), vmem, vmem, vmem, vmem, vmem, vmem, hbm, hbm],
         out_specs=vmem,
         out_shape=jax.ShapeDtypeStruct((token_count, features), jnp.bfloat16),
         scratch_shapes=[
@@ -454,7 +469,7 @@
         compiler_params=pltpu.CompilerParams(
             collective_id=1, has_side_effects=True, vmem_limit_bytes=50 * 2**20
         ),
-    )(counts, q, grads, aux_rows, rows, cols, keys, values)
+    )(counts, q, grads, first, aux_rows, rows, cols, keys, values)
 
 
 def grad_kernel(groups, capacity, scale, counts, q, g, aux, rows, cols, keys, values, out, total):
@@ -540,7 +555,7 @@
     base = jnp.pad(base, ((0, 0), (0, LANES - heads * AUX)))
 
     if groups == 4 and heads == 4 and lax.axis_size("pb") == 8:
-        grads, aux_rows, all_queries, rows, cols = readout(
+        grads, first, aux_rows, all_queries, rows, cols = readout(
             readout_grad,
             readout_weight,
             outputs,
@@ -552,7 +567,7 @@
             heads,
             width,
         )
-        return attend(counts, all_queries, grads, aux_rows, rows, cols, cluster_keys, values, capacity, scale)
+        return attend(counts, all_queries, grads, first, aux_rows, rows, cols, cluster_keys, values, capacity, scale)
 
     probe_lanes = probes.transpose(1, 0, 2).reshape(token_count, heads * probes.shape[2])
     probe_lanes = jnp.pad(probe_lanes, ((0, 0), (0, LANES - probe_lanes.shape[1]))).astype(jnp.bfloat16)

time: 139 us -> 139 us (level)
    pallas_call x1, Pallas kernels: 49.6 us -> 61.9 us  [readout(): pl.pallas_call(functools.partial(readout_kernel, groups, heads, width), i...]
    pallas_call x1, Pallas kernels: 83.2 us -> 71.5 us  [attend(): pl.pallas_call(functools.partial(attend_kernel, groups, capacity, scale),...]
where the time goes in v5:
time: 139 us
  Pallas kernels  133 us (96%)
  local copies, waits for them, and re-layouts  3.99 us (3%)
  other arithmetic  1.61 us (1%)
    pallas_call x1, Pallas kernels, attend(): pl.pallas_call(functools.partial(attend_kernel, groups, capacity, scale),...  71.5 us
    pallas_call x1, Pallas kernels, readout(): pl.pallas_call(functools.partial(readout_kernel, groups, heads, width), i...  61.9 us
    unnamed x7, local copies, waits for them, and re-layouts  2.88 us

profile of v5, /device:TPU:0, one launch (start us, length us, event | category | flops | bytes accessed | tf_op | source)
XLA Modules:
  0.0 139.1 jit_solution(2734935268077693629)
XLA Ops:
  0.0 0.9 select_reduce_fusion
  0.9 0.1 reshape.17.named
  1.0 0.7 reduce-precision_subtract_fusion
  1.7 0.8 reshape.15.probes
  2.5 0.1 concatenate.3
  2.6 0.1 copy.21
  2.8 0.0 copy-start.1
  2.8 1.0 copy-done.1
  3.8 0.0 copy-start.2
  3.8 1.0 copy-done.2
  4.9 0.0 copy-start
  4.9 61.9 %shard_map.100 = (bf16[256,512]{1,0:T(8,128)(2,1)S(1)}, bf16[4,256,512]{2,1,0:T(8,128)(2,1)S(1)}, bf16[32,512]{1,0:T(8,128)(2,1)S(1)}, bf16[4,512,512]{2,1,0:T(8...) custom-call(bf16[512,1024]{1,0:T(8,128)(2,1)} %r.1, bf16[512,8192]{1,0:T(8,128)(2,1)} %w.1, ...), custom_call_target="tpu_custom_call" | custom-call | flops 4294967296 | bytes 33554432 | tf_op jit(solution)/shard_map/pallas_call | solution.py:268
  66.7 0.0 copy-done
  66.7 71.5 %shard_map.101 = bf16[512,512]{1,0:T(8,128)(2,1)S(1)} custom-call(s32[4,8]{1,0:T(4,128)S(1)} %copy-done, bf16[4,512,512]{2,1,0:T(8,128)(2,1)} %get-tuple-element.11.q, bf16[256,512]{1,0:T(8,128)(2,1)S(1)} %get-tuple-element.12.grads, bf16[4,256,512]{2,1,0:T(8,128)(2,1)S(1)} %get-tuple-element.13.first, bf16[32,512]{1,0:T(8,128)(2,1)S(1)} %get-tuple-element.14.aux_rows, ...), custom_call_target="tpu_custom_call" | custom-call | tf_op jit(solution)/shard_map/pallas_call | solution.py:447
  138.3 0.8 copy.24
  (7 shorter events, 0.1 us)
Async XLA Ops:
  2.8 1.0 copy-start.1
  3.8 1.0 copy-start.2
  4.9 61.9 %copy-start = (s32[4,8]{1,0:T(4,128)S(1)}, s32[4,8]{1,0:T(4,128)}, u32[]{:S(2)}) copy-start(s32[4,8]{1,0:T(4,128)} %counts.1) | copy-start | bytes 388
